TPU v7x, 128 devices: a whole 4x4x4 slice. The times are simulated.
128 devices in a mesh: dp: 16 (over x_lo, z, core), expert: 8 (over x_hi, y).
Axes of the slice: x: 4 (x_hi: 2, x_lo: 2; x = x_hi * 2 + x_lo), y: 4, z: 4, core: 2. Of those that a mesh axis runs over, the one named last changes fastest.
Arguments:
- tokens: bfloat16 [2048, 3072], P(('dp', 'expert')), may hold values from -6 to 6
- router_weight: bfloat16 [8, 3072], replicated, may hold values from -0.109375 to 0.109375
- expert_ids: int32 [2048, 2], P(('dp', 'expert')), may hold values from 0 to 7, all different within a row; in each aligned block of 16 rows (0 to 15, 16 to 31, ...) at most 8 rows name the same one
- w_gate: bfloat16 [8, 3072, 8192], P('expert', None, 'dp'), may hold values from -0.109375 to 0.109375
- w_up: bfloat16 [8, 3072, 8192], P('expert', None, 'dp'), may hold values from -0.109375 to 0.109375
- w_down: bfloat16 [8, 8192, 3072], P('expert', 'dp'), may hold values from -0.0625 to 0.0625
- grad_out: bfloat16 [2048, 3072], P(('dp', 'expert')), may hold values from -6 to 6
Outputs:
- mixed: bfloat16 [2048, 3072], P(('dp', 'expert'))
- grad_tokens: bfloat16 [2048, 3072], P(('dp', 'expert'))
- grad_router: float32 [8, 3072], replicated
- grad_gate: bfloat16 [8, 3072, 8192], P('expert', None, 'dp')
- grad_up: bfloat16 [8, 3072, 8192], P('expert', None, 'dp')
- grad_down: bfloat16 [8, 8192, 3072], P('expert', 'dp')
Inputs may be any that keep to these rules, and one draw needn't show every extreme that they name: `expert_ids`: the two experts of a token differ; among the rows of one device no expert is named more than 8 times; every expert is named by some row.
All inputs are finite; a program needn't handle non-finite values.
Results may differ from a plain program's by a relative error of at most 0.024.
Values may be sent and summed in bfloat16 or wider, within the bound.
No kernel may reach another device: no remote copies, remote signals or barrier semaphores. Data moves between devices by JAX's collectives and lax.ppermute only.
A program may use at most 128 MiB of HBM per device.

v0:
```python
import jax
import jax.numpy as jnp
from jax import lax
from jax.sharding import Mesh, PartitionSpec as P

CAP = 8
HIGHEST = lax.Precision.HIGHEST
BF16 = jnp.bfloat16
F32 = jnp.float32

AXES = ("xl", "z", "c", "xh", "y")
CHIPS = ("xl", "z")
OWNERS = ("xh", "y")
HOLDERS = ("xl", "z", "c")
EVERY = ("xl", "z", "xh", "y")


def flip_perm(size, bit):
    return [(k, k ^ bit) for k in range(size)]


def slot_tables(route_ids, experts):
    count = route_ids.shape[0]
    place = jnp.arange(count, dtype=jnp.int32)
    earlier = place[None, :] < place[:, None]
    column = jnp.arange(experts * CAP, dtype=jnp.int32)
    tables = []
    for k in range(2):
        own = route_ids[:, k]
        rank = sum(
            jnp.sum((earlier & (own[:, None] == route_ids[:, m][None, :])).astype(jnp.int32), axis=1)
            for m in range(2)
        )
        tables.append((column[:, None] == (own * CAP + rank)[None, :]).astype(F32))
    return tables


def contract_rows(left_side, right_side):
    return lax.dot_general(
        left_side, right_side, (((0,), (0,)), ((), ())), preferred_element_type=F32
    )


def contract_cols(left_side, right_side):
    return lax.dot_general(
        left_side, right_side, (((1,), (1,)), ((), ())), preferred_element_type=F32
    )


def swap_cores(rows):
    return lax.ppermute(rows, "c", [(0, 1), (1, 0)])


def tie(value, *before):
    nothing = sum(b[(0,) * b.ndim].astype(F32) * 0.0 for b in before)
    return value + nothing.astype(value.dtype)


def exchange(rows, experts, width):
    return lax.all_to_all(
        rows.reshape(experts, CAP, width), OWNERS, split_axis=0, concat_axis=0, tiled=True
    ).reshape(experts * CAP, width)


def of_core(rows, core):
    blocks = rows.reshape(8, 2, -1, rows.shape[-1])
    picked = lax.dynamic_index_in_dim(blocks, core, axis=1, keepdims=False)
    return picked.reshape(-1, rows.shape[-1])


def send_home(merged, experts, width):
    parts = lax.all_to_all(
        merged.reshape(8 * experts, CAP, width), EVERY, split_axis=0, concat_axis=0, tiled=True
    )
    total = parts.reshape(8, experts * CAP, width).astype(F32).sum(axis=0)
    return total.astype(BF16)


def all_sum(part):
    for axis, size, bit in (
        ("c", 2, 1),
        ("z", 4, 1),
        ("z", 4, 2),
        ("y", 4, 1),
        ("y", 4, 2),
        ("xl", 2, 1),
        ("xh", 2, 1),
    ):
        part = part + lax.ppermute(part, axis, flip_perm(size, bit))
    return part


def on_device(tokens, router_weight, expert_ids, w_gate, w_up, w_down, grad_out):
    tok_count, model_width = tokens.shape
    experts = router_weight.shape[0]
    slot_count = experts * CAP
    first_table, second_table = slot_tables(expert_ids, experts)
    token_table = (first_table + second_table).astype(BF16)
    placed = jnp.dot(
        token_table, tokens, preferred_element_type=F32
    ).astype(BF16)
    arrived = exchange(placed, experts, model_width)

    logits = contract_cols(tokens, router_weight)
    expert_range = jnp.arange(experts, dtype=jnp.int32)
    first_hot = (expert_ids[:, 0:1] == expert_range[None, :]).astype(F32)
    second_hot = (expert_ids[:, 1:2] == expert_range[None, :]).astype(F32)
    first_logit = jnp.sum(logits * first_hot, axis=1)
    second_logit = jnp.sum(logits * second_hot, axis=1)
    share_first = jax.nn.sigmoid(first_logit - second_logit)
    share_second = jax.nn.sigmoid(second_logit - first_logit)
    cotangent = grad_out.astype(F32)
    slot_share = jnp.sum(first_table * share_first + second_table * share_second, axis=1)
    placed_grads = jnp.dot(token_table, grad_out, preferred_element_type=F32)
    placed_grads = (placed_grads * tie(slot_share, arrived)[:, None]).astype(BF16)
    grad_arrived = exchange(placed_grads, experts, model_width)

    gathered = lax.all_gather(arrived, HOLDERS, axis=0, tiled=True)
    grad_gathered = lax.all_gather(grad_arrived, HOLDERS, axis=0, tiled=True)
    core = lax.axis_index("c")

    gate_matrix = w_gate[0]
    up_matrix = w_up[0]
    down_matrix = w_down[0]
    pre_gate = jnp.dot(gathered, gate_matrix, preferred_element_type=F32)
    pre_up = jnp.dot(gathered, up_matrix, preferred_element_type=F32)
    gate_sigmoid = jax.nn.sigmoid(pre_gate)
    gate_silu = pre_gate * gate_sigmoid
    hidden = tie(gate_silu * pre_up, grad_arrived).astype(BF16)
    out_theirs = jnp.dot(
        of_core(hidden, 1 - core), down_matrix, preferred_element_type=F32
    ).astype(BF16)
    out_other = swap_cores(out_theirs)
    out_mine = jnp.dot(of_core(hidden, core), down_matrix, preferred_element_type=F32)
    out_merged = (out_mine + out_other.astype(F32)).astype(BF16)
    returned = send_home(out_merged, experts, model_width)
    hidden_grad = tie(contract_cols(grad_gathered, down_matrix), out_merged)
    silu_slope = gate_sigmoid * (1.0 + pre_gate * (1.0 - gate_sigmoid))
    up_grad = (hidden_grad * gate_silu).astype(BF16)
    gate_grad = (hidden_grad * pre_up * silu_slope).astype(BF16)

    def back(which):
        return contract_cols(of_core(gate_grad, which), gate_matrix) + contract_cols(
            of_core(up_grad, which), up_matrix
        )

    back_other = swap_cores(back(1 - core).astype(BF16))
    back_mine = back(core)
    grad_down = contract_rows(hidden, grad_gathered).astype(BF16)[None]
    grad_gate = contract_rows(gathered, gate_grad).astype(BF16)[None]
    grad_up = contract_rows(gathered, up_grad).astype(BF16)[None]
    back_home = send_home(
        tie(
            back_mine + back_other.astype(F32), returned, grad_down, grad_gate, grad_up
        ).astype(BF16), experts, model_width
    )
    home = returned
    first_out = contract_rows(first_table.astype(BF16), home)
    second_out = contract_rows(second_table.astype(BF16), home)
    mixed = (share_first[:, None] * first_out + share_second[:, None] * second_out).astype(
        BF16
    )
    both_back = contract_rows((first_table + second_table).astype(BF16), back_home)
    dshare_first = jnp.sum(cotangent * first_out, axis=1)
    dshare_second = jnp.sum(cotangent * second_out, axis=1)
    logit_step = (dshare_first - dshare_second) * share_first * share_second
    logit_grad = logit_step[:, None] * (first_hot - second_hot)
    router_back = jnp.dot(logit_grad, router_weight.astype(F32), precision=HIGHEST)
    grad_tokens = (both_back + router_back).astype(BF16)
    local_router = lax.dot_general(
        logit_grad,
        tokens.astype(F32),
        (((0,), (0,)), ((), ())),
        precision=HIGHEST,
        preferred_element_type=F32,
    )
    grad_router = all_sum(local_router)
    return (mixed, grad_tokens, grad_router, grad_gate, grad_up, grad_down)


def solution(mesh):
    fine = Mesh(mesh.devices.reshape(2, 4, 2, 2, 4), AXES)
    dp = ("xl", "z", "c")
    rows = P(AXES, None)
    return jax.shard_map(
        on_device,
        mesh=fine,
        in_specs=(
            rows,
            P(),
            rows,
            P(OWNERS, None, dp),
            P(OWNERS, None, dp),
            P(OWNERS, dp, None),
            rows,
        ),
        out_specs=(
            rows,
            rows,
            P(),
            P(OWNERS, None, dp),
            P(OWNERS, None, dp),
            P(OWNERS, dp, None),
        ),
        check_vma=False,
    )
```

profile of v0, /device:TPU:24, one launch (start us, length us, event | category | flops | bytes accessed | tf_op | source)
XLA Modules:
  0.0 291.8 jit_solution(11223505870858946255)
XLA Ops:
  7.2 0.9 slice_bitcast_fusion.1
  8.1 0.2 convert_reduce_fusion.2
  8.3 0.8 add_add_fusion.1
  9.1 1.2 fusion.6
  10.3 15.1 %all_to_all.20 = bf16[8,8,3072]{2,1,0:T(8,128)(2,1)} all-to-all(bf16[8,8,3072]{2,1,0:T(8,128)(2,1)S(1)} %fusion.6), channel_id=1, replica_groups=mesh['xl'=2,'z'=4,'c'=2,'xh'=2,'y'=4] {'xh','y'}, dimensions={0} | all-to-all | bytes 786432 | tf_op jit(solution)/shard_map/all_to_all | solution.py:60
  25.4 0.0 all-gather.5.cloned.1.call-start
  25.5 1.0 select_reduce_fusion.1
  26.6 0.1 add_reduce_fusion
  26.7 1.2 slice.42
  28.5 1.2 fusion.5
  29.8 16.6 %all_to_all.21 = bf16[8,8,3072]{2,1,0:T(8,128)(2,1)} all-to-all(bf16[8,8,3072]{2,1,0:T(8,128)(2,1)S(1)} %fusion.5), channel_id=1, replica_groups=mesh['xl'=2,'z'=4,'c'=2,'xh'=2,'y'=4] {'xh','y'}, dimensions={0} | all-to-all | bytes 786432 | tf_op jit(solution)/shard_map/all_to_all | solution.py:60
  46.4 1.1 slice.43
  48.2 22.6 %all-gather.3.cloned.1.call-done = bf16[1024,3072]{1,0:T(8,128)(2,1)} async-done(((bf16[64,3072]{1,0:T(8,128)(2,1)}), bf16[1024,3072]{1,0:T(8,128)(2,1)}) %all-gather.3.cloned.1.call-update) | async-done | bytes 6291472 | tf_op jit(solution)/shard_map/all_gather | solution.py:118
  70.8 6.6 %fusion.23 = f32[1024,512]{1,0:T(8,128)S(1)} fusion(bf16[1024,3072]{1,0:T(8,128)(2,1)} %all-gather.3.cloned.1.call-done, bf16[1,3072,512]{2,1,0:T(8,128)(2,1)} %param.10), kind=kOutput, calls=%fused_computation.33 | convolution fusion | flops 3221225472 | bytes 11534336 | tf_op jit(solution)/shard_map/dot_general | solution.py:125
  77.4 4.9 %add_convert_fusion.3 = (bf16[1024,512]{1,0:T(8,128)(2,1)S(1)}, f32[1024,512]{1,0:T(8,128)}) fusion(f32[]{:T(128)} %bitcast.9, f32[1024,512]{1,0:T(8,128)S(1)} %fusion.23, bf16[1024,3072]{1,0:T(8,128)(2,1)S(1)} %copy-done.12, bf16[1,3072,512]{2,1,0:T(8,128)(2,1)S(1)} %copy-done.4), kind=kOutput, calls=%fused_computation.37 | convolution fusion | flops 3224895488 | bytes 14680068 | tf_op jit(solution)/shard_map/dot_general | solution.py:126
  82.3 0.1 constant_dynamic-slice_fusion.5
  82.4 1.9 convolution_convert_fusion.3
  84.2 0.3 collective-permute-start
  84.6 5.4 %collective-permute-done = bf16[512,3072]{1,0:T(8,128)(2,1)S(1)} collective-permute-done((bf16[512,3072]{1,0:T(8,128)(2,1)S(1)}, bf16[512,3072]{1,0:T(8,128)(2,1)S(1)}, u32[]{:S(2)}, u32[]{:S(2)}) %collective-permute-start) | collective-permute-done | bytes 3145760 | tf_op jit(solution)/shard_map/ppermute | solution.py:51
  90.0 1.8 add_convert_fusion.2
  91.8 0.6 slice.44
  92.4 1.1 copy-done.3
  93.5 11.1 %all-to-all-start.2 = ((bf16[64,8,3072]{2,1,0:T(8,128)(2,1)}), bf16[64,8,3072]{2,1,0:T(8,128)(2,1)}, u32[]{:S(2)}, u32[]{:S(2)}) async-start(bf16[64,8,3072]{2,1,0:T(8,128)(2,1)} %bitcast.96), calls=%async_computation.2 | async-start | bytes 6291456 | tf_op jit(solution)/shard_map/all_to_all | solution.py:72
  105.2 45.1 %all-gather.5.cloned.1.call-done = bf16[1024,3072]{1,0:T(8,128)(2,1)} async-done(((bf16[64,3072]{1,0:T(8,128)(2,1)}), bf16[1024,3072]{1,0:T(8,128)(2,1)}) %all-gather.5.cloned.1.call-update) | async-done | bytes 6291472 | tf_op jit(solution)/shard_map/all_gather | solution.py:119
  150.3 7.6 %multiply_convert_fusion = (bf16[1024,512]{1,0:T(8,128)(2,1)S(1)}, bf16[1024,512]{1,0:T(8,128)(2,1)S(1)}) fusion(f32[]{:T(128)} %bitcast.16, f32[1024,512]{1,0:T(8,128)} %copy-done.16, f32[1024,512]{1,0:T(8,128)} %get-tuple-element.30, bf16[1024,3072]{1,0:T(8,128)(2,1)} %all-gather.5.cloned.1.call-done, bf16[1,512,3072]{2,1,0:T(8,128)(2,1)S(1)} %copy-done), kind=kOutput, calls=%fused_computation.35 | convolution fusion | flops 3228565504 | bytes 15728644 | tf_op jit(solution)/shard_map/dot_general | solution.py:45
  158.0 1.0 constant_dynamic-slice_fusion.2
  159.0 1.1 copy-done.2
  160.1 1.8 fusion.19
  161.9 0.1 copy-done.5
  162.0 3.5 %add_convert_fusion.1 = bf16[512,3072]{1,0:T(8,128)(2,1)} fusion(f32[512,3072]{1,0:T(8,128)S(1)} %fusion.19, bf16[512,512]{1,0:T(8,128)(2,1)S(1)} %bitcast.98, bf16[1,3072,512]{2,1,0:T(8,128)(2,1)S(1)} %copy-done.5), kind=kOutput, calls=%fused_computation.1 | convolution fusion | flops 1613758464 | bytes 13107200 | tf_op jit(solution)/shard_map/dot_general | solution.py:45
  165.5 0.2 collective-permute-start.1
  165.7 3.8 %fusion = bf16[1,512,3072]{2,1,0:T(8,128)(2,1)S(1)} fusion(bf16[1024,512]{1,0:T(8,128)(2,1)S(1)} %copy-done.7, bf16[1024,3072]{1,0:T(8,128)(2,1)S(1)} %bitcast.113), kind=kOutput, calls=%fused_computation.7 | convolution fusion | flops 3222798336 | bytes 10485760 | tf_op jit(solution)/shard_map/dot_general | solution.py:39
  169.5 0.6 slice.46
  170.8 3.8 %fusion.1 = bf16[1,3072,512]{2,1,0:T(8,128)(2,1)S(1)} fusion(bf16[1024,3072]{1,0:T(8,128)(2,1)S(1)} %bitcast.111, bf16[1024,512]{1,0:T(8,128)(2,1)S(1)} %get-tuple-element.15), kind=kOutput, calls=%fused_computation.8 | convolution fusion | flops 3222798336 | bytes 10485760 | tf_op jit(solution)/shard_map/dot_general | solution.py:39
  174.6 0.6 slice.47
  175.8 3.8 %fusion.2 = bf16[1,3072,512]{2,1,0:T(8,128)(2,1)S(1)} fusion(bf16[1024,3072]{1,0:T(8,128)(2,1)S(1)} %bitcast.111, bf16[1024,512]{1,0:T(8,128)(2,1)S(1)} %get-tuple-element.14), kind=kOutput, calls=%fused_computation.9 | convolution fusion | flops 3222798336 | bytes 10485760 | tf_op jit(solution)/shard_map/dot_general | solution.py:39
  179.6 0.6 slice.48
  180.8 0.4 copy-done.15
  181.2 4.5 %fusion.21 = f32[512,3072]{1,0:T(8,128)} fusion(bf16[512,512]{1,0:T(8,128)(2,1)S(1)} %bitcast.97, bf16[1,3072,512]{2,1,0:T(8,128)(2,1)S(1)} %copy-done.2), kind=kOutput, calls=%fused_computation.31 | convolution fusion | flops 1610612736 | bytes 9961472 | tf_op jit(solution)/shard_map/dot_general | solution.py:45
  185.8 2.4 bitcast_reduce_fusion.1
  188.2 0.5 slice.45
  189.4 8.3 %fusion.3 = bf16[64,8,3072]{2,1,0:T(8,128)(2,1)} fusion(bf16[512,3072]{1,0:T(8,128)(2,1)} %collective-permute-done.1, f32[512,3072]{1,0:T(8,128)} %fusion.21, bf16[512,512]{1,0:T(8,128)(2,1)S(1)} %bitcast.107, bf16[1,3072,512]{2,1,0:T(8,128)(2,1)} %param.11, f32[]{:T(128)S(6)} %add.182), kind=kOutput, calls=%fused_computation.10 | convolution fusion | flops 1618477056 | bytes 16252932 | tf_op jit(solution)/shard_map/dot_general | solution.py:45
  197.8 15.1 %all-to-all-start.3 = ((bf16[64,8,3072]{2,1,0:T(8,128)(2,1)}), bf16[64,8,3072]{2,1,0:T(8,128)(2,1)}, u32[]{:S(2)}, u32[]{:S(2)}) async-start(bf16[64,8,3072]{2,1,0:T(8,128)(2,1)} %fusion.3), calls=%async_computation.3 | async-start | bytes 6291456 | tf_op jit(solution)/shard_map/all_to_all | solution.py:72
  212.9 0.2 fusion.36
  213.1 1.0 fusion.27
  214.2 0.2 fusion.38
  214.3 0.1 collective-permute-start.2
  214.4 1.3 collective-permute-done.2
  215.7 1.5 collective-permute-start.3
  217.3 29.7 %collective-permute-done.3 = f32[8,3072]{1,0:T(8,128)S(1)} collective-permute-done((f32[8,3072]{1,0:T(8,128)S(1)}, f32[8,3072]{1,0:T(8,128)S(1)}, u32[]{:S(2)}, u32[]{:S(2)}) %collective-permute-start.3) | collective-permute-done | bytes 98336 | tf_op jit(solution)/shard_map/ppermute | solution.py:89
  246.9 7.7 %collective-permute-start.4 = (f32[8,3072]{1,0:T(8,128)S(1)}, f32[8,3072]{1,0:T(8,128)S(1)}, u32[]{:S(2)}, u32[]{:S(2)}) collective-permute-start(f32[8,3072]{1,0:T(8,128)S(1)} %add.187), channel_id=1, source_target_pairs={{0,32},{16,48},{32,0},{48,16},{1,33},{17,49},{33,1},{49,17},{2,34}... | collective-permute-start | bytes 294920 | tf_op jit(solution)/shard_map/ppermute | solution.py:89
  254.6 3.1 %collective-permute-done.4 = f32[8,3072]{1,0:T(8,128)S(1)} collective-permute-done((f32[8,3072]{1,0:T(8,128)S(1)}, f32[8,3072]{1,0:T(8,128)S(1)}, u32[]{:S(2)}, u32[]{:S(2)}) %collective-permute-start.4) | collective-permute-done | bytes 98336 | tf_op jit(solution)/shard_map/ppermute | solution.py:89
  257.7 1.9 collective-permute-start.5
  259.6 2.8 collective-permute-done.5
  262.4 2.3 collective-permute-start.6
  264.7 3.9 %collective-permute-done.6 = f32[8,3072]{1,0:T(8,128)S(1)} collective-permute-done((f32[8,3072]{1,0:T(8,128)S(1)}, f32[8,3072]{1,0:T(8,128)S(1)}, u32[]{:S(2)}, u32[]{:S(2)}) %collective-permute-start.6) | collective-permute-done | bytes 98336 | tf_op jit(solution)/shard_map/ppermute | solution.py:89
  268.7 2.3 collective-permute-start.7
  270.9 2.6 collective-permute-done.7
  273.5 4.8 %collective-permute-start.8 = (f32[8,3072]{1,0:T(8,128)S(1)}, f32[8,3072]{1,0:T(8,128)S(1)}, u32[]{:S(2)}, u32[]{:S(2)}) collective-permute-start(f32[8,3072]{1,0:T(8,128)S(1)} %add.191), channel_id=1, source_target_pairs={{0,4},{4,0},{1,5},{5,1},{2,6},{6,2},{3,7},{7,3},{8,12},{12,8},{9,1... | collective-permute-start | bytes 294920 | tf_op jit(solution)/shard_map/ppermute | solution.py:89
  278.4 0.3 fusion.39
  278.7 2.3 collective-permute-done.8
  281.0 0.7 add.192
  281.6 2.4 bitcast_reduce_fusion
  284.0 0.9 fusion.7
  (55 shorter events, 0.3 us)
Async XLA Ops:
  7.2 75.2 %copy-start = (bf16[1,512,3072]{2,1,0:T(8,128)(2,1)S(1)}, bf16[1,512,3072]{2,1,0:T(8,128)(2,1)}, u32[]{:S(2)}) copy-start(bf16[1,512,3072]{2,1,0:T(8,128)(2,1)} %param.12) | copy-start | bytes 9437188
  7.2 63.6 %all-gather.3.cloned.1.call-start = ((), (), s32[]{:S(2)}) async-start(), calls=%async_computation.4 | async-start | bytes 6684672 | tf_op jit(solution)/shard_map/all_gather | solution.py:118
  25.4 124.9 %all-gather.5.cloned.1.call-start = ((), (), s32[]{:S(2)}) async-start(), calls=%async_computation.5 | async-start | bytes 6684672 | tf_op jit(solution)/shard_map/all_gather | solution.py:119
  70.8 6.6 %copy-start.4 = (bf16[1,3072,512]{2,1,0:T(8,128)(2,1)S(1)}, bf16[1,3072,512]{2,1,0:T(8,128)(2,1)}, u32[]{:S(2)}) copy-start(bf16[1,3072,512]{2,1,0:T(8,128)(2,1)} %param.11) | copy-start | bytes 9437188
  70.8 6.6 %copy-start.12 = (bf16[1024,3072]{1,0:T(8,128)(2,1)S(1)}, bf16[1024,3072]{1,0:T(8,128)(2,1)}, u32[]{:S(2)}) copy-start(bf16[1024,3072]{1,0:T(8,128)(2,1)} %all-gather.3.cloned.1.call-done) | copy-start | bytes 18874372
  77.4 4.9 %copy-start.16 = (f32[1024,512]{1,0:T(8,128)}, f32[1024,512]{1,0:T(8,128)S(1)}, u32[]{:S(2)}) copy-start(f32[1024,512]{1,0:T(8,128)S(1)} %fusion.23) | copy-start | bytes 6291460
  82.3 1.9 copy-start.6
  84.2 5.7 %collective-permute-start = (bf16[512,3072]{1,0:T(8,128)(2,1)S(1)}, bf16[512,3072]{1,0:T(8,128)(2,1)S(1)}, u32[]{:S(2)}, u32[]{:S(2)}) collective-permute-start(bf16[512,3072]{1,0:T(8,128)(2,1)S(1)} %convolution_convert_fusion.3), channel_id=1, source_target_pairs={{0,8},{8,0},{1,9},{9,1},{2,10},{10,2},{3,11},{11,3},{4,12},{12,4},... | collective-permute-start | bytes 9437192 | tf_op jit(solution)/shard_map/ppermute | solution.py:51
  91.8 1.7 copy-start.3
  93.5 92.3 %all-to-all-start.2 = ((bf16[64,8,3072]{2,1,0:T(8,128)(2,1)}), bf16[64,8,3072]{2,1,0:T(8,128)(2,1)}, u32[]{:S(2)}, u32[]{:S(2)}) async-start(bf16[64,8,3072]{2,1,0:T(8,128)(2,1)} %bitcast.96), calls=%async_computation.2 | async-start | bytes 6291456 | tf_op jit(solution)/shard_map/all_to_all | solution.py:72
  158.0 2.1 copy-start.2
  160.1 1.9 copy-start.5
  160.1 5.7 %slice-start.2 = ((s8[6291456]{0:T(1024)(128)(4,1)}), s8[4194304]{0:T(1024)(128)(4,1)S(1)}, s32[]{:S(2)}) async-start(s8[6291456]{0:T(1024)(128)(4,1)} %bitcast.112), calls=%async_computation.8 | async-start | bytes 8388608
  162.0 3.8 %copy-start.7 = (bf16[1024,512]{1,0:T(8,128)(2,1)S(1)}, bf16[1024,512]{1,0:T(8,128)(2,1)}, u32[]{:S(2)}) copy-start(bf16[1024,512]{1,0:T(8,128)(2,1)} %copy-done.6) | copy-start | bytes 3145732
  162.0 3.8 %slice-start.3 = ((s8[6291456]{0:T(1024)(128)(4,1)}), s8[2097152]{0:T(1024)(128)(4,1)S(1)}, s32[]{:S(2)}) async-start(s8[6291456]{0:T(1024)(128)(4,1)} %bitcast.112), calls=%async_computation.9 | async-start | bytes 4194304
  162.0 8.8 %slice-start = ((s8[6291456]{0:T(1024)(128)(4,1)}), s8[4194304]{0:T(1024)(128)(4,1)S(1)}, s32[]{:S(2)}) async-start(s8[6291456]{0:T(1024)(128)(4,1)} %bitcast.110), calls=%async_computation.6 | async-start | bytes 8388608
  165.5 5.3 %slice-start.1 = ((s8[6291456]{0:T(1024)(128)(4,1)}), s8[2097152]{0:T(1024)(128)(4,1)S(1)}, s32[]{:S(2)}) async-start(s8[6291456]{0:T(1024)(128)(4,1)} %bitcast.110), calls=%async_computation.7 | async-start | bytes 4194304
  165.5 23.9 %collective-permute-start.1 = (bf16[512,3072]{1,0:T(8,128)(2,1)}, bf16[512,3072]{1,0:T(8,128)(2,1)}, u32[]{:S(2)}, u32[]{:S(2)}) collective-permute-start(bf16[512,3072]{1,0:T(8,128)(2,1)} %add_convert_fusion.1), channel_id=1, source_target_pairs={{0,8},{8,0},{1,9},{9,1},{2,10},{10,2},{3,11},{11,3},{4,12},{12,4},... | collective-permute-start | bytes 9437192 | tf_op jit(solution)/shard_map/ppermute | solution.py:51
  169.5 5.0 %copy-start.13 = (bf16[1,512,3072]{2,1,0:T(8,128)(2,1)}, bf16[1,512,3072]{2,1,0:T(8,128)(2,1)S(1)}, u32[]{:S(2)}) copy-start(bf16[1,512,3072]{2,1,0:T(8,128)(2,1)S(1)} %fusion) | copy-start | bytes 9437188
  174.6 5.0 %copy-start.14 = (bf16[1,3072,512]{2,1,0:T(8,128)(2,1)}, bf16[1,3072,512]{2,1,0:T(8,128)(2,1)S(1)}, u32[]{:S(2)}) copy-start(bf16[1,3072,512]{2,1,0:T(8,128)(2,1)S(1)} %fusion.1) | copy-start | bytes 9437188
  179.6 1.7 copy-start.15
  185.8 3.6 %copy-start.9 = (bf16[8,1,64,512]{3,2,1,0:T(8,128)(2,1)S(1)}, bf16[8,1,64,512]{3,2,1,0:T(8,128)(2,1)}, u32[]{:S(2)}) copy-start(bf16[8,1,64,512]{3,2,1,0:T(8,128)(2,1)} %get-tuple-element.16) | copy-start | bytes 1572868
  197.8 15.4 %copy-start.10 = (bf16[16,3072]{1,0:T(8,128)(2,1)S(1)}, bf16[16,3072]{1,0:T(8,128)(2,1)}, u32[]{:S(2)}) copy-start(bf16[16,3072]{1,0:T(8,128)(2,1)} %param.13) | copy-start | bytes 294916
  197.8 16.4 %copy-start.8 = (bf16[16,3072]{1,0:T(8,128)(2,1)S(1)}, bf16[16,3072]{1,0:T(8,128)(2,1)}, u32[]{:S(2)}) copy-start(bf16[16,3072]{1,0:T(8,128)(2,1)} %param.7) | copy-start | bytes 294916
  197.8 83.9 %all-to-all-start.3 = ((bf16[64,8,3072]{2,1,0:T(8,128)(2,1)}), bf16[64,8,3072]{2,1,0:T(8,128)(2,1)}, u32[]{:S(2)}, u32[]{:S(2)}) async-start(bf16[64,8,3072]{2,1,0:T(8,128)(2,1)} %fusion.3), calls=%async_computation.3 | async-start | bytes 6291456 | tf_op jit(solution)/shard_map/all_to_all | solution.py:72
  212.9 65.5 %copy-start.11 = (bf16[8,3072]{1,0:T(8,128)(2,1)S(1)}, bf16[8,3072]{1,0:T(8,128)(2,1)}, u32[]{:S(2)}) copy-start(bf16[8,3072]{1,0:T(8,128)(2,1)} %param.8) | copy-start | bytes 147460
  214.3 1.4 collective-permute-start.2
  215.7 69.2 %copy-start.1 = (bf16[1,512,3072]{2,1,0:T(8,128)(2,1)S(1)}, bf16[1,512,3072]{2,1,0:T(8,128)(2,1)}, u32[]{:S(2)}) copy-start(bf16[1,512,3072]{2,1,0:T(8,128)(2,1)} %param.12) | copy-start | bytes 9437188
  215.7 31.2 %collective-permute-start.3 = (f32[8,3072]{1,0:T(8,128)S(1)}, f32[8,3072]{1,0:T(8,128)S(1)}, u32[]{:S(2)}, u32[]{:S(2)}) collective-permute-start(f32[8,3072]{1,0:T(8,128)S(1)} %add.186), channel_id=1, source_target_pairs={{0,16},{16,0},{32,48},{48,32},{1,17},{17,1},{33,49},{49,33},{2,18}... | collective-permute-start | bytes 294920 | tf_op jit(solution)/shard_map/ppermute | solution.py:89
  246.9 10.8 %collective-permute-start.4 = (f32[8,3072]{1,0:T(8,128)S(1)}, f32[8,3072]{1,0:T(8,128)S(1)}, u32[]{:S(2)}, u32[]{:S(2)}) collective-permute-start(f32[8,3072]{1,0:T(8,128)S(1)} %add.187), channel_id=1, source_target_pairs={{0,32},{16,48},{32,0},{48,16},{1,33},{17,49},{33,1},{49,17},{2,34}... | collective-permute-start | bytes 294920 | tf_op jit(solution)/shard_map/ppermute | solution.py:89
  257.7 4.7 %collective-permute-start.5 = (f32[8,3072]{1,0:T(8,128)S(1)}, f32[8,3072]{1,0:T(8,128)S(1)}, u32[]{:S(2)}, u32[]{:S(2)}) collective-permute-start(f32[8,3072]{1,0:T(8,128)S(1)} %add.188), channel_id=1, source_target_pairs={{0,1},{1,0},{2,3},{3,2},{4,5},{5,4},{6,7},{7,6},{8,9},{9,8},{10,11... | collective-permute-start | bytes 294920 | tf_op jit(solution)/shard_map/ppermute | solution.py:89
  262.4 6.2 %collective-permute-start.6 = (f32[8,3072]{1,0:T(8,128)S(1)}, f32[8,3072]{1,0:T(8,128)S(1)}, u32[]{:S(2)}, u32[]{:S(2)}) collective-permute-start(f32[8,3072]{1,0:T(8,128)S(1)} %add.189), channel_id=1, source_target_pairs={{0,2},{1,3},{2,0},{3,1},{4,6},{5,7},{6,4},{7,5},{8,10},{9,11},{10,... | collective-permute-start | bytes 294920 | tf_op jit(solution)/shard_map/ppermute | solution.py:89
  268.7 4.9 %collective-permute-start.7 = (f32[8,3072]{1,0:T(8,128)S(1)}, f32[8,3072]{1,0:T(8,128)S(1)}, u32[]{:S(2)}, u32[]{:S(2)}) collective-permute-start(f32[8,3072]{1,0:T(8,128)S(1)} %add.190), channel_id=1, source_target_pairs={{0,64},{64,0},{1,65},{65,1},{2,66},{66,2},{3,67},{67,3},{4,68},{68... | collective-permute-start | bytes 294920 | tf_op jit(solution)/shard_map/ppermute | solution.py:89
  273.5 7.4 %collective-permute-start.8 = (f32[8,3072]{1,0:T(8,128)S(1)}, f32[8,3072]{1,0:T(8,128)S(1)}, u32[]{:S(2)}, u32[]{:S(2)}) collective-permute-start(f32[8,3072]{1,0:T(8,128)S(1)} %add.191), channel_id=1, source_target_pairs={{0,4},{4,0},{1,5},{5,1},{2,6},{6,2},{3,7},{7,3},{8,12},{12,8},{9,1... | collective-permute-start | bytes 294920 | tf_op jit(solution)/shard_map/ppermute | solution.py:89
Sparse Core Ops, SparseCore 0:
  25.6 45.1 all-gather.2
  72.5 77.8 all-gather.4
where the time goes:
time: 293 us; the launch traced here: 292 us
  waiting for transfers between devices  119 us (41%)
  matrix products  58.3 us (20%)
  starting transfers between devices  47.4 us (16%)
  blocking collectives  31.7 us (11%)
  between operations  19.1 us (7%)
  local copies, waits for them, and re-layouts  9.74 us (3%)
  other arithmetic  6.66 us (2%)
    ppermute x7, waiting for transfers between devices, all_sum(): part = part + lax.ppermute(part, axis, flip_perm(size, bit))  45.7 us
    all_gather x1, waiting for transfers between devices, on_device(): grad_gathered = lax.all_gather(grad_arrived, HOLDERS, axis=0, tiled=True)  45.1 us
    all_to_all x2, blocking collectives, exchange(): lax.all_to_all(rows.reshape(experts, CAP, width), OWNERS, split_axis=0, c...  31.7 us
    dot_general x6, matrix products, contract_cols(): lax.dot_general(left_side, right_side, (((1,), (1,)), ((), ())), preferre...  26.9 us
    all_to_all x2, starting transfers between devices, send_home(): lax.all_to_all(merged.reshape(8 * experts, CAP, width), EVERY, split_axis...  26.2 us
    all_gather x1, waiting for transfers between devices, on_device(): gathered = lax.all_gather(arrived, HOLDERS, axis=0, tiled=True)  22.6 us
    ppermute x7, starting transfers between devices, all_sum(): part = part + lax.ppermute(part, axis, flip_perm(size, bit))  20.6 us
    dot_general x6, matrix products, contract_rows(): lax.dot_general(left_side, right_side, (((0,), (0,)), ((), ())), preferre...  13.4 us
  transfers between devices with their start and end apart: 13, of which 10 were waited for; matrix products, arithmetic and copies ran while one was open for 20% of the time, Pallas kernels for 0%

commit v1 on v0

--- a/solution.py
+++ b/solution.py
@@ -77,16 +77,10 @@
 
 
 def all_sum(part):
-    for axis, size, bit in (
-        ("c", 2, 1),
-        ("z", 4, 1),
-        ("z", 4, 2),
-        ("y", 4, 1),
-        ("y", 4, 2),
-        ("xl", 2, 1),
-        ("xh", 2, 1),
-    ):
-        part = part + lax.ppermute(part, axis, flip_perm(size, bit))
+    part = part + lax.ppermute(part, "c", flip_perm(2, 1))
+    for axis in ("z", "y", ("xl", "xh")):
+        one, two, three = (lax.ppermute(part, axis, flip_perm(4, bit)) for bit in (1, 2, 3))
+        part = (part + one) + (two + three)
     return part
 
 
@@ -145,28 +139,21 @@
         )
 
     back_other = swap_cores(back(1 - core).astype(BF16))
-    back_mine = back(core)
+    back_mine = lax.optimization_barrier(back(core).astype(BF16))
     grad_down = contract_rows(hidden, grad_gathered).astype(BF16)[None]
     grad_gate = contract_rows(gathered, gate_grad).astype(BF16)[None]
     grad_up = contract_rows(gathered, up_grad).astype(BF16)[None]
-    back_home = send_home(
-        tie(
-            back_mine + back_other.astype(F32), returned, grad_down, grad_gate, grad_up
-        ).astype(BF16), experts, model_width
-    )
     home = returned
     first_out = contract_rows(first_table.astype(BF16), home)
     second_out = contract_rows(second_table.astype(BF16), home)
     mixed = (share_first[:, None] * first_out + share_second[:, None] * second_out).astype(
         BF16
     )
-    both_back = contract_rows((first_table + second_table).astype(BF16), back_home)
     dshare_first = jnp.sum(cotangent * first_out, axis=1)
     dshare_second = jnp.sum(cotangent * second_out, axis=1)
     logit_step = (dshare_first - dshare_second) * share_first * share_second
     logit_grad = logit_step[:, None] * (first_hot - second_hot)
     router_back = jnp.dot(logit_grad, router_weight.astype(F32), precision=HIGHEST)
-    grad_tokens = (both_back + router_back).astype(BF16)
     local_router = lax.dot_general(
         logit_grad,
         tokens.astype(F32),
@@ -175,6 +162,13 @@
         preferred_element_type=F32,
     )
     grad_router = all_sum(local_router)
+    back_home = send_home(
+        tie(
+            back_mine.astype(F32) + back_other.astype(F32), grad_router
+        ).astype(BF16), experts, model_width
+    )
+    both_back = contract_rows((first_table + second_table).astype(BF16), back_home)
+    grad_tokens = (both_back + router_back).astype(BF16)
     return (mixed, grad_tokens, grad_router, grad_gate, grad_up, grad_down)
 
 

time: 293 us -> 260 us (0.89)
  waiting for transfers between devices: 119 us -> 99 us
  starting transfers between devices: 47.4 us -> 37 us
    ppermute x7 -> x10, waiting for transfers between devices: 45.7 us -> 9.77 us  [the longest x9 9.77 us: all_sum(): lax.ppermute(part, axis, flip_perm(4, bit))]
    all_to_all x2, waiting for transfers between devices: 0.01 us -> 17.3 us  [send_home(): lax.all_to_all(merged.reshape(8 * experts, CAP, width), EVERY, split_axis...]
    dot_general x6, matrix products: 26.9 us -> 16 us  [contract_cols(): lax.dot_general(left_side, right_side, (((1,), (1,)), ((), ())), preferre...]
    dot_general x6, matrix products: 13.4 us -> 22.7 us  [contract_rows(): lax.dot_general(left_side, right_side, (((0,), (0,)), ((), ())), preferre...]
    ppermute x7 -> x10, starting transfers between devices: 20.6 us -> 14.9 us  [the longest x9 14.4 us: all_sum(): lax.ppermute(part, axis, flip_perm(4, bit))]
    all_to_all x2, starting transfers between devices: 26.2 us -> 21.6 us  [send_home(): lax.all_to_all(merged.reshape(8 * experts, CAP, width), EVERY, split_axis...]
  transfers between devices with their start and end apart: 13 -> 16, of which waited for: 10 -> 10; matrix products, arithmetic and copies ran while one was open for 20% -> 23% of each run, Pallas kernels for 0% -> 0%
where the time goes in v1:
time: 260 us
  waiting for transfers between devices  99 us (38%)
  matrix products  58.5 us (22%)
  starting transfers between devices  37 us (14%)
  blocking collectives  31.7 us (12%)
  between operations  17 us (7%)
  other arithmetic  8.98 us (3%)
  local copies, waits for them, and re-layouts  7.71 us (3%)
    all_gather x1, waiting for transfers between devices, on_device(): grad_gathered = lax.all_gather(grad_arrived, HOLDERS, axis=0, tiled=True)  43.9 us
    all_to_all x2, blocking collectives, exchange(): lax.all_to_all(rows.reshape(experts, CAP, width), OWNERS, split_axis=0, c...  31.7 us
    dot_general x6, matrix products, contract_rows(): lax.dot_general(left_side, right_side, (((0,), (0,)), ((), ())), preferre...  22.7 us
    all_gather x1, waiting for transfers between devices, on_device(): gathered = lax.all_gather(arrived, HOLDERS, axis=0, tiled=True)  22.6 us
    all_to_all x2, starting transfers between devices, send_home(): lax.all_to_all(merged.reshape(8 * experts, CAP, width), EVERY, split_axis...  21.6 us
    all_to_all x2, waiting for transfers between devices, send_home(): lax.all_to_all(merged.reshape(8 * experts, CAP, width), EVERY, split_axis...  17.3 us
    dot_general x6, matrix products, contract_cols(): lax.dot_general(left_side, right_side, (((1,), (1,)), ((), ())), preferre...  16 us
    ppermute x9, starting transfers between devices, all_sum(): lax.ppermute(part, axis, flip_perm(4, bit))  14.4 us
  transfers between devices with their start and end apart: 16, of which 10 were waited for; matrix products, arithmetic and copies ran while one was open for 23% of the time, Pallas kernels for 0%

profile of v1, /device:TPU:24, one launch (start us, length us, event | category | flops | bytes accessed | tf_op | source)
XLA Modules:
  0.0 259.8 jit_solution(3326183347584563316)
XLA Ops:
  7.2 0.0 all-gather.3.cloned.1.call-start
  7.2 0.9 slice_bitcast_fusion.1
  8.1 0.2 convert_reduce_fusion.2
  8.3 0.8 add_add_fusion.4
  9.1 1.2 fusion.5
  10.3 15.1 %all_to_all.20 = bf16[8,8,3072]{2,1,0:T(8,128)(2,1)} all-to-all(bf16[8,8,3072]{2,1,0:T(8,128)(2,1)S(1)} %fusion.5), channel_id=1, replica_groups=mesh['xl'=2,'z'=4,'c'=2,'xh'=2,'y'=4] {'xh','y'}, dimensions={0} | all-to-all | bytes 786432 | tf_op jit(solution)/shard_map/all_to_all | solution.py:60
  25.4 0.0 all-gather.3.cloned.1.call-update
  25.4 0.0 all-gather.5.cloned.1.call-start
  25.5 1.0 select_reduce_fusion.1
  26.6 0.1 add_reduce_fusion
  26.7 1.2 slice.30
  28.5 1.2 fusion.4
  29.8 16.6 %all_to_all.21 = bf16[8,8,3072]{2,1,0:T(8,128)(2,1)} all-to-all(bf16[8,8,3072]{2,1,0:T(8,128)(2,1)S(1)} %fusion.4), channel_id=1, replica_groups=mesh['xl'=2,'z'=4,'c'=2,'xh'=2,'y'=4] {'xh','y'}, dimensions={0} | all-to-all | bytes 786432 | tf_op jit(solution)/shard_map/all_to_all | solution.py:60
  46.4 0.0 all-gather.5.cloned.1.call-update
  46.4 1.1 slice.31
  48.2 22.6 %all-gather.3.cloned.1.call-done = bf16[1024,3072]{1,0:T(8,128)(2,1)} async-done(((bf16[64,3072]{1,0:T(8,128)(2,1)}), bf16[1024,3072]{1,0:T(8,128)(2,1)}) %all-gather.3.cloned.1.call-update) | async-done | bytes 6291472 | tf_op jit(solution)/shard_map/all_gather | solution.py:112
  70.8 6.6 %fusion.23 = f32[1024,512]{1,0:T(8,128)S(1)} fusion(bf16[1024,3072]{1,0:T(8,128)(2,1)} %all-gather.3.cloned.1.call-done, bf16[1,3072,512]{2,1,0:T(8,128)(2,1)} %param.10), kind=kOutput, calls=%fused_computation.34 | convolution fusion | flops 3221225472 | bytes 11534336 | tf_op jit(solution)/shard_map/dot_general | solution.py:119
  77.4 4.9 %add_convert_fusion.4 = (bf16[1024,512]{1,0:T(8,128)(2,1)S(1)}, f32[1024,512]{1,0:T(8,128)}) fusion(f32[]{:T(128)} %bitcast.9, f32[1024,512]{1,0:T(8,128)S(1)} %fusion.23, bf16[1024,3072]{1,0:T(8,128)(2,1)S(1)} %copy-done.19, bf16[1,3072,512]{2,1,0:T(8,128)(2,1)S(1)} %copy-done.3), kind=kOutput, calls=%fused_computation.38 | convolution fusion | flops 3224895488 | bytes 14680068 | tf_op jit(solution)/shard_map/dot_general | solution.py:120
  82.3 0.1 constant_dynamic-slice_fusion.5
  82.4 1.9 convolution_convert_fusion.3
  84.2 0.3 collective-permute-start
  84.6 5.4 %collective-permute-done = bf16[512,3072]{1,0:T(8,128)(2,1)S(1)} collective-permute-done((bf16[512,3072]{1,0:T(8,128)(2,1)S(1)}, bf16[512,3072]{1,0:T(8,128)(2,1)S(1)}, u32[]{:S(2)}, u32[]{:S(2)}) %collective-permute-start) | collective-permute-done | bytes 3145760 | tf_op jit(solution)/shard_map/ppermute | solution.py:51
  90.0 3.5 %add_convert_fusion.3 = bf16[512,3072]{1,0:T(8,128)(2,1)} fusion(bf16[512,3072]{1,0:T(8,128)(2,1)S(1)} %collective-permute-done, bf16[512,512]{1,0:T(8,128)(2,1)S(1)} %bitcast.105, bf16[1,512,3072]{2,1,0:T(8,128)(2,1)S(1)} %copy-done), kind=kOutput, calls=%fused_computation.3 | convolution fusion | flops 1615331328 | bytes 9961472 | tf_op jit(solution)/shard_map/dot_general | solution.py:128
  93.5 11.1 %all-to-all-start.2 = ((bf16[64,8,3072]{2,1,0:T(8,128)(2,1)}), bf16[64,8,3072]{2,1,0:T(8,128)(2,1)}, u32[]{:S(2)}, u32[]{:S(2)}) async-start(bf16[64,8,3072]{2,1,0:T(8,128)(2,1)} %bitcast.93), calls=%async_computation.2 | async-start | bytes 6291456 | tf_op jit(solution)/shard_map/all_to_all | solution.py:72
  104.5 1.2 slice.32
  106.4 43.9 %all-gather.5.cloned.1.call-done = bf16[1024,3072]{1,0:T(8,128)(2,1)} async-done(((bf16[64,3072]{1,0:T(8,128)(2,1)}), bf16[1024,3072]{1,0:T(8,128)(2,1)}) %all-gather.5.cloned.1.call-update) | async-done | bytes 6291472 | tf_op jit(solution)/shard_map/all_gather | solution.py:113
  150.3 7.6 %multiply_convert_fusion = (bf16[1024,512]{1,0:T(8,128)(2,1)S(1)}, bf16[1024,512]{1,0:T(8,128)(2,1)S(1)}) fusion(f32[]{:T(128)} %bitcast.16, f32[1024,512]{1,0:T(8,128)} %copy-done.20, f32[1024,512]{1,0:T(8,128)} %get-tuple-element.30, bf16[1024,3072]{1,0:T(8,128)(2,1)} %all-gather.5.cloned.1.call-done, bf16[1,512,3072]{2,1,0:T(8,128)(2,1)S(1)} %copy-done), kind=kOutput, calls=%fused_computation.36 | convolution fusion | flops 3228565504 | bytes 15728644 | tf_op jit(solution)/shard_map/dot_general | solution.py:45
  158.0 0.9 copy-done.9
  159.0 0.3 copy-done.11
  159.3 1.3 constant_dynamic-slice_fusion.2
  160.7 2.5 bitcast_reduce_fusion.1
  163.2 0.2 fusion.36
  163.4 1.0 fusion.27
  164.5 0.2 fusion.39
  164.7 0.5 collective-permute-start.2
  165.2 1.8 fusion.19
  167.0 3.8 %collective-permute-start.5 = (f32[8,3072]{1,0:T(8,128)S(1)}, f32[8,3072]{1,0:T(8,128)S(1)}, u32[]{:S(2)}, u32[]{:S(2)}) collective-permute-start(f32[8,3072]{1,0:T(8,128)S(1)} %add.180), channel_id=1, source_target_pairs={{0,48},{16,32},{32,16},{48,0},{1,49},{17,33},{33,17},{49,1},{2,50}... | collective-permute-start | bytes 294920 | tf_op jit(solution)/shard_map/ppermute | solution.py:82
  170.8 0.5 collective-permute-start.4
  171.4 0.4 collective-permute-start.3
  171.8 1.8 add_convert_fusion.1
  173.6 0.1 collective-permute-start.1
  173.7 1.7 collective-permute-done.5
  175.5 2.5 collective-permute-done.4
  178.0 3.9 %collective-permute-start.8 = (f32[8,3072]{1,0:T(8,128)S(1)}, f32[8,3072]{1,0:T(8,128)S(1)}, u32[]{:S(2)}, u32[]{:S(2)}) collective-permute-start(f32[8,3072]{1,0:T(8,128)S(1)} %add_add_fusion.2), channel_id=1, source_target_pairs={{0,3},{1,2},{2,1},{3,0},{4,7},{5,6},{6,5},{7,4},{8,11},{9,10},{10,... | collective-permute-start | bytes 294920 | tf_op jit(solution)/shard_map/ppermute | solution.py:82
  182.0 0.9 collective-permute-start.6
  182.9 1.9 fusion.21
  184.8 0.8 collective-permute-done.8
  185.6 2.5 collective-permute-done.7
  188.1 2.6 %collective-permute-start.11 = (f32[8,3072]{1,0:T(8,128)S(1)}, f32[8,3072]{1,0:T(8,128)S(1)}, u32[]{:S(2)}, u32[]{:S(2)}) collective-permute-start(f32[8,3072]{1,0:T(8,128)S(1)} %add_add_fusion.1), channel_id=1, source_target_pairs={{0,68},{4,64},{64,4},{68,0},{1,69},{5,65},{65,5},{69,1},{2,70},{6,... | collective-permute-start | bytes 294920 | tf_op jit(solution)/shard_map/ppermute | solution.py:82
  190.8 0.1 collective-permute-start.10
  190.8 2.1 collective-permute-start.9
  192.9 1.8 add_convert_fusion.2
  194.7 0.6 collective-permute-done.10
  195.4 1.6 collective-permute-done.9
  197.0 0.5 slice.33
  198.2 2.9 %fusion.7 = bf16[64,8,3072]{2,1,0:T(8,128)(2,1)} fusion(bf16[512,3072]{1,0:T(8,128)(2,1)S(1)} %collective-permute-done.1, bf16[512,3072]{1,0:T(8,128)(2,1)S(1)} %add_convert_fusion.2, f32[]{:T(128)} %bitcast.23), kind=kLoop, calls=%fused_computation.18 | loop fusion | flops 7864320 | bytes 9437188 | tf_op jit(solution)/shard_map/reshape | solution.py:73
  201.0 10.5 %all-to-all-start.3 = ((bf16[64,8,3072]{2,1,0:T(8,128)(2,1)}), bf16[64,8,3072]{2,1,0:T(8,128)(2,1)}, u32[]{:S(2)}, u32[]{:S(2)}) async-start(bf16[64,8,3072]{2,1,0:T(8,128)(2,1)} %fusion.7), calls=%async_computation.3 | async-start | bytes 6291456 | tf_op jit(solution)/shard_map/all_to_all | solution.py:72
  211.5 7.8 %fusion.2 = bf16[1,512,3072]{2,1,0:T(8,128)(2,1)} fusion(bf16[1024,512]{1,0:T(8,128)(2,1)S(1)} %copy-done.14, bf16[1024,3072]{1,0:T(8,128)(2,1)} %all-gather.5.cloned.1.call-done), kind=kOutput, calls=%fused_computation.10 | convolution fusion | flops 3222798336 | bytes 10485760 | tf_op jit(solution)/shard_map/dot_general | solution.py:39
  219.3 7.9 %fusion.1 = bf16[1,3072,512]{2,1,0:T(8,128)(2,1)} fusion(bf16[1024,3072]{1,0:T(8,128)(2,1)} %all-gather.3.cloned.1.call-done, bf16[1024,512]{1,0:T(8,128)(2,1)S(1)} %copy-done.12), kind=kOutput, calls=%fused_computation.9 | convolution fusion | flops 3222798336 | bytes 10485760 | tf_op jit(solution)/shard_map/dot_general | solution.py:39
  227.3 4.9 %fusion = bf16[1,3072,512]{2,1,0:T(8,128)(2,1)} fusion(bf16[1024,3072]{1,0:T(8,128)(2,1)S(1)} %bitcast.108, bf16[1024,512]{1,0:T(8,128)(2,1)S(1)} %copy-done.10), kind=kOutput, calls=%fused_computation.8 | convolution fusion | flops 3222798336 | bytes 10485760 | tf_op jit(solution)/shard_map/dot_general | solution.py:39
  232.2 0.3 fusion.38
  232.5 17.3 %all-to-all-done.3 = bf16[64,8,3072]{2,1,0:T(8,128)(2,1)} async-done(((bf16[64,8,3072]{2,1,0:T(8,128)(2,1)}), bf16[64,8,3072]{2,1,0:T(8,128)(2,1)}, u32[]{:S(2)}, u32[]{:S(2)}) %all-to-all-start.3) | async-done | bytes 3145760 | tf_op jit(solution)/shard_map/all_to_all | solution.py:72
  249.7 2.4 bitcast_reduce_fusion
  252.1 0.9 fusion.6
  (59 shorter events, 0.2 us)
Async XLA Ops:
  7.2 75.2 %copy-start = (bf16[1,512,3072]{2,1,0:T(8,128)(2,1)S(1)}, bf16[1,512,3072]{2,1,0:T(8,128)(2,1)}, u32[]{:S(2)}) copy-start(bf16[1,512,3072]{2,1,0:T(8,128)(2,1)} %param.12) | copy-start | bytes 9437188
  7.2 63.6 %all-gather.3.cloned.1.call-start = ((), (), s32[]{:S(2)}) async-start(), calls=%async_computation.4 | async-start | bytes 6684672 | tf_op jit(solution)/shard_map/all_gather | solution.py:112
  25.4 124.9 %all-gather.5.cloned.1.call-start = ((), (), s32[]{:S(2)}) async-start(), calls=%async_computation.5 | async-start | bytes 6684672 | tf_op jit(solution)/shard_map/all_gather | solution.py:113
  70.8 6.6 %copy-start.3 = (bf16[1,3072,512]{2,1,0:T(8,128)(2,1)S(1)}, bf16[1,3072,512]{2,1,0:T(8,128)(2,1)}, u32[]{:S(2)}) copy-start(bf16[1,3072,512]{2,1,0:T(8,128)(2,1)} %param.11) | copy-start | bytes 9437188
  70.8 6.6 %copy-start.19 = (bf16[1024,3072]{1,0:T(8,128)(2,1)S(1)}, bf16[1024,3072]{1,0:T(8,128)(2,1)}, u32[]{:S(2)}) copy-start(bf16[1024,3072]{1,0:T(8,128)(2,1)} %all-gather.3.cloned.1.call-done) | copy-start | bytes 18874372
  77.4 4.9 %copy-start.20 = (f32[1024,512]{1,0:T(8,128)}, f32[1024,512]{1,0:T(8,128)S(1)}, u32[]{:S(2)}) copy-start(f32[1024,512]{1,0:T(8,128)S(1)} %fusion.23) | copy-start | bytes 6291460
  82.3 1.9 copy-start.13
  84.2 5.7 %collective-permute-start = (bf16[512,3072]{1,0:T(8,128)(2,1)S(1)}, bf16[512,3072]{1,0:T(8,128)(2,1)S(1)}, u32[]{:S(2)}, u32[]{:S(2)}) collective-permute-start(bf16[512,3072]{1,0:T(8,128)(2,1)S(1)} %convolution_convert_fusion.3), channel_id=1, source_target_pairs={{0,8},{8,0},{1,9},{9,1},{2,10},{10,2},{3,11},{11,3},{4,12},{12,4},... | collective-permute-start | bytes 9437192 | tf_op jit(solution)/shard_map/ppermute | solution.py:51
  93.5 67.2 %all-to-all-start.2 = ((bf16[64,8,3072]{2,1,0:T(8,128)(2,1)}), bf16[64,8,3072]{2,1,0:T(8,128)(2,1)}, u32[]{:S(2)}, u32[]{:S(2)}) async-start(bf16[64,8,3072]{2,1,0:T(8,128)(2,1)} %bitcast.93), calls=%async_computation.2 | async-start | bytes 6291456 | tf_op jit(solution)/shard_map/all_to_all | solution.py:72
  158.0 1.0 copy-start.9
  158.0 1.3 copy-start.11
  159.3 4.1 %copy-start.16 = (bf16[16,3072]{1,0:T(8,128)(2,1)S(1)}, bf16[16,3072]{1,0:T(8,128)(2,1)}, u32[]{:S(2)}) copy-start(bf16[16,3072]{1,0:T(8,128)(2,1)} %param.13) | copy-start | bytes 294916
  160.6 3.8 %copy-start.15 = (bf16[16,3072]{1,0:T(8,128)(2,1)S(1)}, bf16[16,3072]{1,0:T(8,128)(2,1)}, u32[]{:S(2)}) copy-start(bf16[16,3072]{1,0:T(8,128)(2,1)} %param.7) | copy-start | bytes 294916
  160.6 4.5 %copy-start.2 = (bf16[1,3072,512]{2,1,0:T(8,128)(2,1)S(1)}, bf16[1,3072,512]{2,1,0:T(8,128)(2,1)}, u32[]{:S(2)}) copy-start(bf16[1,3072,512]{2,1,0:T(8,128)(2,1)} %param.10) | copy-start | bytes 9437188
  160.7 4.5 %copy-start.8 = (bf16[8,1,64,512]{3,2,1,0:T(8,128)(2,1)S(1)}, bf16[8,1,64,512]{3,2,1,0:T(8,128)(2,1)}, u32[]{:S(2)}) copy-start(bf16[8,1,64,512]{3,2,1,0:T(8,128)(2,1)} %get-tuple-element.31) | copy-start | bytes 1572868
  164.7 2.4 collective-permute-start.2
  165.2 6.6 %copy-start.4 = (bf16[1,3072,512]{2,1,0:T(8,128)(2,1)S(1)}, bf16[1,3072,512]{2,1,0:T(8,128)(2,1)}, u32[]{:S(2)}) copy-start(bf16[1,3072,512]{2,1,0:T(8,128)(2,1)} %param.11) | copy-start | bytes 9437188
  165.2 6.6 %copy-start.7 = (bf16[8,1,64,512]{3,2,1,0:T(8,128)(2,1)S(1)}, bf16[8,1,64,512]{3,2,1,0:T(8,128)(2,1)}, u32[]{:S(2)}) copy-start(bf16[8,1,64,512]{3,2,1,0:T(8,128)(2,1)} %get-tuple-element.17) | copy-start | bytes 1572868
  167.0 8.4 %collective-permute-start.5 = (f32[8,3072]{1,0:T(8,128)S(1)}, f32[8,3072]{1,0:T(8,128)S(1)}, u32[]{:S(2)}, u32[]{:S(2)}) collective-permute-start(f32[8,3072]{1,0:T(8,128)S(1)} %add.180), channel_id=1, source_target_pairs={{0,48},{16,32},{32,16},{48,0},{1,49},{17,33},{33,17},{49,1},{2,50}... | collective-permute-start | bytes 294920 | tf_op jit(solution)/shard_map/ppermute | solution.py:82
  170.8 7.2 %collective-permute-start.4 = (f32[8,3072]{1,0:T(8,128)S(1)}, f32[8,3072]{1,0:T(8,128)S(1)}, u32[]{:S(2)}, u32[]{:S(2)}) collective-permute-start(f32[8,3072]{1,0:T(8,128)S(1)} %add.180), channel_id=1, source_target_pairs={{0,32},{16,48},{32,0},{48,16},{1,33},{17,49},{33,1},{49,17},{2,34}... | collective-permute-start | bytes 294920 | tf_op jit(solution)/shard_map/ppermute | solution.py:82
  171.4 6.6 %collective-permute-start.3 = (f32[8,3072]{1,0:T(8,128)S(1)}, f32[8,3072]{1,0:T(8,128)S(1)}, u32[]{:S(2)}, u32[]{:S(2)}) collective-permute-start(f32[8,3072]{1,0:T(8,128)S(1)} %add.180), channel_id=1, source_target_pairs={{0,16},{16,0},{32,48},{48,32},{1,17},{17,1},{33,49},{49,33},{2,18}... | collective-permute-start | bytes 294920 | tf_op jit(solution)/shard_map/ppermute | solution.py:82
  171.8 11.1 %copy-start.6 = (bf16[8,1,64,512]{3,2,1,0:T(8,128)(2,1)S(1)}, bf16[8,1,64,512]{3,2,1,0:T(8,128)(2,1)}, u32[]{:S(2)}) copy-start(bf16[8,1,64,512]{3,2,1,0:T(8,128)(2,1)} %get-tuple-element.32) | copy-start | bytes 1572868
  173.6 24.5 %collective-permute-start.1 = (bf16[512,3072]{1,0:T(8,128)(2,1)S(1)}, bf16[512,3072]{1,0:T(8,128)(2,1)S(1)}, u32[]{:S(2)}, u32[]{:S(2)}) collective-permute-start(bf16[512,3072]{1,0:T(8,128)(2,1)S(1)} %add_convert_fusion.1), channel_id=1, source_target_pairs={{0,8},{8,0},{1,9},{9,1},{2,10},{10,2},{3,11},{11,3},{4,12},{12,4},... | collective-permute-start | bytes 9437192 | tf_op jit(solution)/shard_map/ppermute | solution.py:51
  178.0 7.6 %collective-permute-start.8 = (f32[8,3072]{1,0:T(8,128)S(1)}, f32[8,3072]{1,0:T(8,128)S(1)}, u32[]{:S(2)}, u32[]{:S(2)}) collective-permute-start(f32[8,3072]{1,0:T(8,128)S(1)} %add_add_fusion.2), channel_id=1, source_target_pairs={{0,3},{1,2},{2,1},{3,0},{4,7},{5,6},{6,5},{7,4},{8,11},{9,10},{10,... | collective-permute-start | bytes 294920 | tf_op jit(solution)/shard_map/ppermute | solution.py:82
  182.0 6.1 %collective-permute-start.7 = (f32[8,3072]{1,0:T(8,128)S(1)}, f32[8,3072]{1,0:T(8,128)S(1)}, u32[]{:S(2)}, u32[]{:S(2)}) collective-permute-start(f32[8,3072]{1,0:T(8,128)S(1)} %add_add_fusion.2), channel_id=1, source_target_pairs={{0,2},{1,3},{2,0},{3,1},{4,6},{5,7},{6,4},{7,5},{8,10},{9,11},{10,... | collective-permute-start | bytes 294920 | tf_op jit(solution)/shard_map/ppermute | solution.py:82
  182.0 6.1 %collective-permute-start.6 = (f32[8,3072]{1,0:T(8,128)S(1)}, f32[8,3072]{1,0:T(8,128)S(1)}, u32[]{:S(2)}, u32[]{:S(2)}) collective-permute-start(f32[8,3072]{1,0:T(8,128)S(1)} %add_add_fusion.2), channel_id=1, source_target_pairs={{0,1},{1,0},{2,3},{3,2},{4,5},{5,4},{6,7},{7,6},{8,9},{9,8},{10,11... | collective-permute-start | bytes 294920 | tf_op jit(solution)/shard_map/ppermute | solution.py:82
  182.9 10.0 %copy-start.5 = (bf16[8,1,64,512]{3,2,1,0:T(8,128)(2,1)S(1)}, bf16[8,1,64,512]{3,2,1,0:T(8,128)(2,1)}, u32[]{:S(2)}) copy-start(bf16[8,1,64,512]{3,2,1,0:T(8,128)(2,1)} %get-tuple-element.16) | copy-start | bytes 1572868
  188.1 6.6 %collective-permute-start.11 = (f32[8,3072]{1,0:T(8,128)S(1)}, f32[8,3072]{1,0:T(8,128)S(1)}, u32[]{:S(2)}, u32[]{:S(2)}) collective-permute-start(f32[8,3072]{1,0:T(8,128)S(1)} %add_add_fusion.1), channel_id=1, source_target_pairs={{0,68},{4,64},{64,4},{68,0},{1,69},{5,65},{65,5},{69,1},{2,70},{6,... | collective-permute-start | bytes 294920 | tf_op jit(solution)/shard_map/ppermute | solution.py:82
  190.8 4.6 %collective-permute-start.10 = (f32[8,3072]{1,0:T(8,128)S(1)}, f32[8,3072]{1,0:T(8,128)S(1)}, u32[]{:S(2)}, u32[]{:S(2)}) collective-permute-start(f32[8,3072]{1,0:T(8,128)S(1)} %add_add_fusion.1), channel_id=1, source_target_pairs={{0,64},{4,68},{64,0},{68,4},{1,65},{5,69},{65,1},{69,5},{2,66},{6,... | collective-permute-start | bytes 294920 | tf_op jit(solution)/shard_map/ppermute | solution.py:82
  190.8 6.1 %collective-permute-start.9 = (f32[8,3072]{1,0:T(8,128)S(1)}, f32[8,3072]{1,0:T(8,128)S(1)}, u32[]{:S(2)}, u32[]{:S(2)}) collective-permute-start(f32[8,3072]{1,0:T(8,128)S(1)} %add_add_fusion.1), channel_id=1, source_target_pairs={{0,4},{4,0},{64,68},{68,64},{1,5},{5,1},{65,69},{69,65},{2,6},{6,2... | collective-permute-start | bytes 294920 | tf_op jit(solution)/shard_map/ppermute | solution.py:82
  196.9 4.1 %copy-start.18 = (f32[8,3072]{1,0:T(8,128)}, f32[8,3072]{1,0:T(8,128)S(1)}, u32[]{:S(2)}) copy-start(f32[8,3072]{1,0:T(8,128)S(1)} %add_add_fusion) | copy-start | bytes 294916
  201.0 10.5 %copy-start.14 = (bf16[1024,512]{1,0:T(8,128)(2,1)S(1)}, bf16[1024,512]{1,0:T(8,128)(2,1)}, u32[]{:S(2)}) copy-start(bf16[1024,512]{1,0:T(8,128)(2,1)} %copy-done.13) | copy-start | bytes 3145732
  201.0 48.7 %all-to-all-start.3 = ((bf16[64,8,3072]{2,1,0:T(8,128)(2,1)}), bf16[64,8,3072]{2,1,0:T(8,128)(2,1)}, u32[]{:S(2)}, u32[]{:S(2)}) async-start(bf16[64,8,3072]{2,1,0:T(8,128)(2,1)} %fusion.7), calls=%async_computation.3 | async-start | bytes 6291456 | tf_op jit(solution)/shard_map/all_to_all | solution.py:72
  211.5 7.8 %copy-start.12 = (bf16[1024,512]{1,0:T(8,128)(2,1)S(1)}, bf16[1024,512]{1,0:T(8,128)(2,1)}, u32[]{:S(2)}) copy-start(bf16[1024,512]{1,0:T(8,128)(2,1)} %copy-done.11) | copy-start | bytes 3145732
  211.5 15.7 %slice-start = ((s8[6291456]{0:T(1024)(128)(4,1)}), s8[4194304]{0:T(1024)(128)(4,1)S(1)}, s32[]{:S(2)}) async-start(s8[6291456]{0:T(1024)(128)(4,1)} %bitcast.107), calls=%async_computation.6 | async-start | bytes 8388608
  219.3 7.9 %copy-start.10 = (bf16[1024,512]{1,0:T(8,128)(2,1)S(1)}, bf16[1024,512]{1,0:T(8,128)(2,1)}, u32[]{:S(2)}) copy-start(bf16[1024,512]{1,0:T(8,128)(2,1)} %copy-done.9) | copy-start | bytes 3145732
  219.3 7.9 %slice-start.1 = ((s8[6291456]{0:T(1024)(128)(4,1)}), s8[2097152]{0:T(1024)(128)(4,1)S(1)}, s32[]{:S(2)}) async-start(s8[6291456]{0:T(1024)(128)(4,1)} %bitcast.107), calls=%async_computation.7 | async-start | bytes 4194304
  227.3 4.9 %copy-start.17 = (bf16[8,3072]{1,0:T(8,128)(2,1)S(1)}, bf16[8,3072]{1,0:T(8,128)(2,1)}, u32[]{:S(2)}) copy-start(bf16[8,3072]{1,0:T(8,128)(2,1)} %param.8) | copy-start | bytes 147460
  227.3 25.7 %copy-start.1 = (bf16[1,512,3072]{2,1,0:T(8,128)(2,1)S(1)}, bf16[1,512,3072]{2,1,0:T(8,128)(2,1)}, u32[]{:S(2)}) copy-start(bf16[1,512,3072]{2,1,0:T(8,128)(2,1)} %param.12) | copy-start | bytes 9437188
Sparse Core Ops, SparseCore 0:
  25.6 45.1 all-gather.2
  72.5 77.8 all-gather.4

commit v2 on v1

--- a/solution.py
+++ b/solution.py
@@ -77,7 +77,6 @@
 
 
 def all_sum(part):
-    part = part + lax.ppermute(part, "c", flip_perm(2, 1))
     for axis in ("z", "y", ("xl", "xh")):
         one, two, three = (lax.ppermute(part, axis, flip_perm(4, bit)) for bit in (1, 2, 3))
         part = (part + one) + (two + three)
@@ -128,21 +127,6 @@
     out_mine = jnp.dot(of_core(hidden, core), down_matrix, preferred_element_type=F32)
     out_merged = (out_mine + out_other.astype(F32)).astype(BF16)
     returned = send_home(out_merged, experts, model_width)
-    hidden_grad = tie(contract_cols(grad_gathered, down_matrix), out_merged)
-    silu_slope = gate_sigmoid * (1.0 + pre_gate * (1.0 - gate_sigmoid))
-    up_grad = (hidden_grad * gate_silu).astype(BF16)
-    gate_grad = (hidden_grad * pre_up * silu_slope).astype(BF16)
-
-    def back(which):
-        return contract_cols(of_core(gate_grad, which), gate_matrix) + contract_cols(
-            of_core(up_grad, which), up_matrix
-        )
-
-    back_other = swap_cores(back(1 - core).astype(BF16))
-    back_mine = lax.optimization_barrier(back(core).astype(BF16))
-    grad_down = contract_rows(hidden, grad_gathered).astype(BF16)[None]
-    grad_gate = contract_rows(gathered, gate_grad).astype(BF16)[None]
-    grad_up = contract_rows(gathered, up_grad).astype(BF16)[None]
     home = returned
     first_out = contract_rows(first_table.astype(BF16), home)
     second_out = contract_rows(second_table.astype(BF16), home)
@@ -161,6 +145,22 @@
         precision=HIGHEST,
         preferred_element_type=F32,
     )
+    local_router = local_router + swap_cores(local_router)
+    hidden_grad = tie(contract_cols(grad_gathered, down_matrix), out_merged, local_router)
+    silu_slope = gate_sigmoid * (1.0 + pre_gate * (1.0 - gate_sigmoid))
+    up_grad = (hidden_grad * gate_silu).astype(BF16)
+    gate_grad = (hidden_grad * pre_up * silu_slope).astype(BF16)
+
+    def back(which):
+        return contract_cols(of_core(gate_grad, which), gate_matrix) + contract_cols(
+            of_core(up_grad, which), up_matrix
+        )
+
+    back_other = swap_cores(back(1 - core).astype(BF16))
+    back_mine = lax.optimization_barrier(back(core).astype(BF16))
+    grad_down = contract_rows(hidden, grad_gathered).astype(BF16)[None]
+    grad_gate = contract_rows(gathered, gate_grad).astype(BF16)[None]
+    grad_up = contract_rows(gathered, up_grad).astype(BF16)[None]
     grad_router = all_sum(local_router)
     back_home = send_home(
         tie(

time: 260 us -> 253 us (0.973)
  blocking collectives: 31.7 us -> 83.4 us
  waiting for transfers between devices: 99 us -> 54.7 us
  starting transfers between devices: 37 us -> 24.3 us
    all_to_all x0 -> x1, blocking collectives: none -> 51.8 us  [send_home(): lax.all_to_all(merged.reshape(8 * experts, CAP, width), EVERY, split_axis...]
    all_gather x1, waiting for transfers between devices: 43.9 us -> 0.02 us  [on_device(): grad_gathered = lax.all_gather(grad_arrived, HOLDERS, axis=0, tiled=True)]
    all_to_all x2 -> x1, starting transfers between devices: 21.6 us -> 8.17 us  [send_home(): lax.all_to_all(merged.reshape(8 * experts, CAP, width), EVERY, split_axis...]
    ppermute x9, waiting for transfers between devices: 9.77 us -> 7.04 us  [all_sum(): lax.ppermute(part, axis, flip_perm(4, bit))]
    all_to_all x2 -> x1, waiting for transfers between devices: 17.3 us -> 18.9 us  [send_home(): lax.all_to_all(merged.reshape(8 * experts, CAP, width), EVERY, split_axis...]
    ppermute x2 -> x3, waiting for transfers between devices: 5.41 us -> 6.18 us  [swap_cores(): return lax.ppermute(rows, 'c', [(0, 1), (1, 0)])]
  transfers between devices with their start and end apart: 16 -> 15, of which waited for: 10 -> 8; matrix products, arithmetic and copies ran while one was open for 23% -> 24% of each run, Pallas kernels for 0% -> 0%
where the time goes in v2:
time: 253 us; the launch traced here: 252 us
  blocking collectives  83.4 us (33%)
  matrix products  56.8 us (22%)
  waiting for transfers between devices  54.7 us (22%)
  starting transfers between devices  24.3 us (10%)
  between operations  17.7 us (7%)
  local copies, waits for them, and re-layouts  7.79 us (3%)
  other arithmetic  6.94 us (3%)
    all_to_all x1, blocking collectives, send_home(): lax.all_to_all(merged.reshape(8 * experts, CAP, width), EVERY, split_axis...  51.8 us
    all_to_all x2, blocking collectives, exchange(): lax.all_to_all(rows.reshape(experts, CAP, width), OWNERS, split_axis=0, c...  31.7 us
    dot_general x6, matrix products, contract_rows(): lax.dot_general(left_side, right_side, (((0,), (0,)), ((), ())), preferre...  22.7 us
    all_gather x1, waiting for transfers between devices, on_device(): gathered = lax.all_gather(arrived, HOLDERS, axis=0, tiled=True)  22.6 us
    all_to_all x1, waiting for transfers between devices, send_home(): lax.all_to_all(merged.reshape(8 * experts, CAP, width), EVERY, split_axis...  18.9 us
    dot_general x6, matrix products, contract_cols(): lax.dot_general(left_side, right_side, (((1,), (1,)), ((), ())), preferre...  16.1 us
    ppermute x9, starting transfers between devices, all_sum(): lax.ppermute(part, axis, flip_perm(4, bit))  15.6 us
    all_to_all x1, starting transfers between devices, send_home(): lax.all_to_all(merged.reshape(8 * experts, CAP, width), EVERY, split_axis...  8.17 us
  transfers between devices with their start and end apart: 15, of which 8 were waited for; matrix products, arithmetic and copies ran while one was open for 24% of the time, Pallas kernels for 0%

profile of v2, /device:TPU:24, one launch (start us, length us, event | category | flops | bytes accessed | tf_op | source)
XLA Modules:
  0.0 251.8 jit_solution(15004129020320817281)
XLA Ops:
  7.2 0.0 all-gather.3.cloned.1.call-start
  7.2 0.9 slice_bitcast_fusion.1
  8.1 0.2 convert_reduce_fusion.2
  8.3 0.8 add_add_fusion.4
  9.1 1.2 fusion.5
  10.3 15.1 %all_to_all.20 = bf16[8,8,3072]{2,1,0:T(8,128)(2,1)} all-to-all(bf16[8,8,3072]{2,1,0:T(8,128)(2,1)S(1)} %fusion.5), channel_id=1, replica_groups=mesh['xl'=2,'z'=4,'c'=2,'xh'=2,'y'=4] {'xh','y'}, dimensions={0} | all-to-all | bytes 786432 | tf_op jit(solution)/shard_map/all_to_all | solution.py:60
  25.4 0.0 all-gather.3.cloned.1.call-update
  25.4 0.0 all-gather.5.cloned.1.call-start
  25.5 1.0 select_reduce_fusion.1
  26.6 0.1 add_reduce_fusion
  26.7 1.2 slice.34
  28.5 1.2 fusion.4
  29.8 16.6 %all_to_all.21 = bf16[8,8,3072]{2,1,0:T(8,128)(2,1)} all-to-all(bf16[8,8,3072]{2,1,0:T(8,128)(2,1)S(1)} %fusion.4), channel_id=1, replica_groups=mesh['xl'=2,'z'=4,'c'=2,'xh'=2,'y'=4] {'xh','y'}, dimensions={0} | all-to-all | bytes 786432 | tf_op jit(solution)/shard_map/all_to_all | solution.py:60
  46.4 1.2 slice.35
  48.2 22.6 %all-gather.3.cloned.1.call-done = bf16[1024,3072]{1,0:T(8,128)(2,1)} async-done(((bf16[64,3072]{1,0:T(8,128)(2,1)}), bf16[1024,3072]{1,0:T(8,128)(2,1)}) %all-gather.3.cloned.1.call-update) | async-done | bytes 6291472 | tf_op jit(solution)/shard_map/all_gather | solution.py:111
  70.8 6.6 %fusion.23 = f32[1024,512]{1,0:T(8,128)S(1)} fusion(bf16[1024,3072]{1,0:T(8,128)(2,1)} %all-gather.3.cloned.1.call-done, bf16[1,3072,512]{2,1,0:T(8,128)(2,1)} %param.10), kind=kOutput, calls=%fused_computation.34 | convolution fusion | flops 3221225472 | bytes 11534336 | tf_op jit(solution)/shard_map/dot_general | solution.py:118
  77.4 4.9 %add_convert_fusion.4 = (bf16[1024,512]{1,0:T(8,128)(2,1)S(1)}, f32[1024,512]{1,0:T(8,128)}) fusion(f32[]{:T(128)} %bitcast.9, f32[1024,512]{1,0:T(8,128)S(1)} %fusion.23, bf16[1024,3072]{1,0:T(8,128)(2,1)S(1)} %copy-done.17, bf16[1,3072,512]{2,1,0:T(8,128)(2,1)S(1)} %copy-done.3), kind=kOutput, calls=%fused_computation.38 | convolution fusion | flops 3224895488 | bytes 14680068 | tf_op jit(solution)/shard_map/dot_general | solution.py:119
  82.3 0.1 constant_dynamic-slice_fusion.5
  82.4 1.8 convolution_convert_fusion.3
  84.2 0.3 collective-permute-start
  84.6 5.4 %collective-permute-done = bf16[512,3072]{1,0:T(8,128)(2,1)S(1)} collective-permute-done((bf16[512,3072]{1,0:T(8,128)(2,1)S(1)}, bf16[512,3072]{1,0:T(8,128)(2,1)S(1)}, u32[]{:S(2)}, u32[]{:S(2)}) %collective-permute-start) | collective-permute-done | bytes 3145760 | tf_op jit(solution)/shard_map/ppermute | solution.py:51
  90.0 1.8 add_convert_fusion.3
  91.8 51.8 %all_to_all.22 = bf16[64,8,3072]{2,1,0:T(8,128)(2,1)S(1)} all-to-all(bf16[64,8,3072]{2,1,0:T(8,128)(2,1)S(1)} %bitcast.94), channel_id=1, replica_groups=mesh['xl'=2,'z'=4,'c'=2,'xh'=2,'y'=4] {'xl','z','xh','y'}, dimensions={0} | all-to-all | bytes 6291456 | tf_op jit(solution)/shard_map/all_to_all | solution.py:72
  143.5 0.5 bitcast_reduce_fusion.1
  144.0 0.2 fusion.36
  144.3 0.2 copy-done.12
  144.4 1.0 fusion.27
  145.5 0.2 fusion.39
  145.6 0.1 collective-permute-start.1
  145.7 0.5 slice.36
  146.2 0.8 collective-permute-done.1
  147.0 0.5 slice.37
  147.5 4.5 %collective-permute-start.5 = (f32[8,3072]{1,0:T(8,128)S(1)}, f32[8,3072]{1,0:T(8,128)S(1)}, u32[]{:S(2)}, u32[]{:S(2)}) collective-permute-start(f32[8,3072]{1,0:T(8,128)S(1)} %add.180), channel_id=1, source_target_pairs={{0,48},{16,32},{32,16},{48,0},{1,49},{17,33},{33,17},{49,1},{2,50}... | collective-permute-start | bytes 294920 | tf_op jit(solution)/shard_map/ppermute | solution.py:81
  152.1 1.6 collective-permute-start.4
  155.0 0.0 all-gather.5.cloned.1.call-done
  155.0 7.6 %multiply_convert_fusion = (bf16[1024,512]{1,0:T(8,128)(2,1)S(1)}, bf16[1024,512]{1,0:T(8,128)(2,1)S(1)}) fusion(f32[]{:T(128)} %bitcast.16, f32[1024,512]{1,0:T(8,128)} %copy-done.18, f32[1024,512]{1,0:T(8,128)} %get-tuple-element.30, bf16[1024,3072]{1,0:T(8,128)(2,1)} %all-gather.5.cloned.1.call-done, bf16[1,512,3072]{2,1,0:T(8,128)(2,1)S(1)} %copy-done), kind=kOutput, calls=%fused_computation.36 | convolution fusion | flops 3228565504 | bytes 15728644 | tf_op jit(solution)/shard_map/dot_general | solution.py:45
  162.7 0.2 constant_dynamic-slice_fusion.2
  162.9 2.4 copy-done.2
  165.3 1.8 fusion.19
  167.2 0.0 copy-done.4
  167.2 1.9 add_convert_fusion.1
  169.2 0.1 collective-permute-start.2
  169.3 2.8 %collective-permute-start.8 = (f32[8,3072]{1,0:T(8,128)S(1)}, f32[8,3072]{1,0:T(8,128)S(1)}, u32[]{:S(2)}, u32[]{:S(2)}) collective-permute-start(f32[8,3072]{1,0:T(8,128)S(1)} %add_add_fusion.2), channel_id=1, source_target_pairs={{0,3},{1,2},{2,1},{3,0},{4,7},{5,6},{6,5},{7,4},{8,11},{9,10},{10,... | collective-permute-start | bytes 294920 | tf_op jit(solution)/shard_map/ppermute | solution.py:81
  172.1 0.6 collective-permute-start.7
  172.6 0.9 collective-permute-start.6
  173.5 1.8 fusion.21
  175.3 1.6 collective-permute-done.8
  176.9 2.3 collective-permute-done.7
  179.2 2.5 %collective-permute-start.11 = (f32[8,3072]{1,0:T(8,128)S(1)}, f32[8,3072]{1,0:T(8,128)S(1)}, u32[]{:S(2)}, u32[]{:S(2)}) collective-permute-start(f32[8,3072]{1,0:T(8,128)S(1)} %add_add_fusion.1), channel_id=1, source_target_pairs={{0,68},{4,64},{64,4},{68,0},{1,69},{5,65},{65,5},{69,1},{2,70},{6,... | collective-permute-start | bytes 294920 | tf_op jit(solution)/shard_map/ppermute | solution.py:81
  181.8 1.6 collective-permute-start.10
  183.4 1.1 collective-permute-start.9
  184.5 1.8 add_convert_fusion.2
  186.3 0.5 collective-permute-done.10
  186.9 2.6 %collective-permute-done.9 = f32[8,3072]{1,0:T(8,128)S(1)} collective-permute-done((f32[8,3072]{1,0:T(8,128)S(1)}, f32[8,3072]{1,0:T(8,128)S(1)}, u32[]{:S(2)}, u32[]{:S(2)}) %collective-permute-start.9) | collective-permute-done | bytes 98336 | tf_op jit(solution)/shard_map/ppermute | solution.py:81
  189.5 0.5 slice.38
  190.7 2.9 %fusion.7 = bf16[64,8,3072]{2,1,0:T(8,128)(2,1)} fusion(bf16[512,3072]{1,0:T(8,128)(2,1)S(1)} %collective-permute-done.2, bf16[512,3072]{1,0:T(8,128)(2,1)S(1)} %add_convert_fusion.2, f32[]{:T(128)} %bitcast.23), kind=kLoop, calls=%fused_computation.18 | loop fusion | flops 7864320 | bytes 9437188 | tf_op jit(solution)/shard_map/reshape | solution.py:73
  193.6 8.2 %all-to-all-start.3 = ((bf16[64,8,3072]{2,1,0:T(8,128)(2,1)}), bf16[64,8,3072]{2,1,0:T(8,128)(2,1)}, u32[]{:S(2)}, u32[]{:S(2)}) async-start(bf16[64,8,3072]{2,1,0:T(8,128)(2,1)} %fusion.7), calls=%async_computation.3 | async-start | bytes 6291456 | tf_op jit(solution)/shard_map/all_to_all | solution.py:72
  201.8 7.8 %fusion.2 = bf16[1,512,3072]{2,1,0:T(8,128)(2,1)} fusion(bf16[1024,512]{1,0:T(8,128)(2,1)S(1)} %copy-done.10, bf16[1024,3072]{1,0:T(8,128)(2,1)} %all-gather.5.cloned.1.call-done), kind=kOutput, calls=%fused_computation.10 | convolution fusion | flops 3222798336 | bytes 10485760 | tf_op jit(solution)/shard_map/dot_general | solution.py:39
  209.6 0.3 fusion.38
  210.0 7.9 %fusion.1 = bf16[1,3072,512]{2,1,0:T(8,128)(2,1)} fusion(bf16[1024,3072]{1,0:T(8,128)(2,1)} %all-gather.3.cloned.1.call-done, bf16[1024,512]{1,0:T(8,128)(2,1)S(1)} %copy-done.8), kind=kOutput, calls=%fused_computation.9 | convolution fusion | flops 3222798336 | bytes 10485760 | tf_op jit(solution)/shard_map/dot_general | solution.py:39
  217.9 4.9 %fusion = bf16[1,3072,512]{2,1,0:T(8,128)(2,1)} fusion(bf16[1024,3072]{1,0:T(8,128)(2,1)S(1)} %bitcast.109, bf16[1024,512]{1,0:T(8,128)(2,1)S(1)} %copy-done.6), kind=kOutput, calls=%fused_computation.8 | convolution fusion | flops 3222798336 | bytes 10485760 | tf_op jit(solution)/shard_map/dot_general | solution.py:39
  222.8 18.9 %all-to-all-done.3 = bf16[64,8,3072]{2,1,0:T(8,128)(2,1)} async-done(((bf16[64,8,3072]{2,1,0:T(8,128)(2,1)}), bf16[64,8,3072]{2,1,0:T(8,128)(2,1)}, u32[]{:S(2)}, u32[]{:S(2)}) %all-to-all-start.3) | async-done | bytes 3145760 | tf_op jit(solution)/shard_map/all_to_all | solution.py:72
  241.7 2.4 bitcast_reduce_fusion
  244.1 0.9 fusion.6
  (55 shorter events, 0.3 us)
Async XLA Ops:
  7.2 75.2 %copy-start = (bf16[1,512,3072]{2,1,0:T(8,128)(2,1)S(1)}, bf16[1,512,3072]{2,1,0:T(8,128)(2,1)}, u32[]{:S(2)}) copy-start(bf16[1,512,3072]{2,1,0:T(8,128)(2,1)} %param.12) | copy-start | bytes 9437188
  7.2 63.6 %all-gather.3.cloned.1.call-start = ((), (), s32[]{:S(2)}) async-start(), calls=%async_computation.4 | async-start | bytes 6684672 | tf_op jit(solution)/shard_map/all_gather | solution.py:111
  25.4 129.6 %all-gather.5.cloned.1.call-start = ((), (), s32[]{:S(2)}) async-start(), calls=%async_computation.5 | async-start | bytes 6684672 | tf_op jit(solution)/shard_map/all_gather | solution.py:112
  70.8 6.6 %copy-start.3 = (bf16[1,3072,512]{2,1,0:T(8,128)(2,1)S(1)}, bf16[1,3072,512]{2,1,0:T(8,128)(2,1)}, u32[]{:S(2)}) copy-start(bf16[1,3072,512]{2,1,0:T(8,128)(2,1)} %param.11) | copy-start | bytes 9437188
  70.8 6.6 %copy-start.17 = (bf16[1024,3072]{1,0:T(8,128)(2,1)S(1)}, bf16[1024,3072]{1,0:T(8,128)(2,1)}, u32[]{:S(2)}) copy-start(bf16[1024,3072]{1,0:T(8,128)(2,1)} %all-gather.3.cloned.1.call-done) | copy-start | bytes 18874372
  77.4 4.9 %copy-start.18 = (f32[1024,512]{1,0:T(8,128)}, f32[1024,512]{1,0:T(8,128)S(1)}, u32[]{:S(2)}) copy-start(f32[1024,512]{1,0:T(8,128)S(1)} %fusion.23) | copy-start | bytes 6291460
  82.3 1.9 copy-start.9
  84.2 5.7 %collective-permute-start = (bf16[512,3072]{1,0:T(8,128)(2,1)S(1)}, bf16[512,3072]{1,0:T(8,128)(2,1)S(1)}, u32[]{:S(2)}, u32[]{:S(2)}) collective-permute-start(bf16[512,3072]{1,0:T(8,128)(2,1)S(1)} %convolution_convert_fusion.3), channel_id=1, source_target_pairs={{0,8},{8,0},{1,9},{9,1},{2,10},{10,2},{3,11},{11,3},{4,12},{12,4},... | collective-permute-start | bytes 9437192 | tf_op jit(solution)/shard_map/ppermute | solution.py:51
  143.5 0.9 copy-start.12
  143.5 1.9 copy-start.11
  145.4 0.8 copy-start.15
  145.6 1.4 collective-permute-start.1
  147.5 21.7 %collective-permute-start.5 = (f32[8,3072]{1,0:T(8,128)S(1)}, f32[8,3072]{1,0:T(8,128)S(1)}, u32[]{:S(2)}, u32[]{:S(2)}) collective-permute-start(f32[8,3072]{1,0:T(8,128)S(1)} %add.180), channel_id=1, source_target_pairs={{0,48},{16,32},{32,16},{48,0},{1,49},{17,33},{33,17},{49,1},{2,50}... | collective-permute-start | bytes 294920 | tf_op jit(solution)/shard_map/ppermute | solution.py:81
  152.1 17.2 %collective-permute-start.4 = (f32[8,3072]{1,0:T(8,128)S(1)}, f32[8,3072]{1,0:T(8,128)S(1)}, u32[]{:S(2)}, u32[]{:S(2)}) collective-permute-start(f32[8,3072]{1,0:T(8,128)S(1)} %add.180), channel_id=1, source_target_pairs={{0,32},{16,48},{32,0},{48,16},{1,33},{17,49},{33,1},{49,17},{2,34}... | collective-permute-start | bytes 294920 | tf_op jit(solution)/shard_map/ppermute | solution.py:81
  153.7 15.6 %collective-permute-start.3 = (f32[8,3072]{1,0:T(8,128)S(1)}, f32[8,3072]{1,0:T(8,128)S(1)}, u32[]{:S(2)}, u32[]{:S(2)}) collective-permute-start(f32[8,3072]{1,0:T(8,128)S(1)} %add.180), channel_id=1, source_target_pairs={{0,16},{16,0},{32,48},{48,32},{1,17},{17,1},{33,49},{49,33},{2,18}... | collective-permute-start | bytes 294920 | tf_op jit(solution)/shard_map/ppermute | solution.py:81
  162.7 4.5 %copy-start.5 = (bf16[1024,512]{1,0:T(8,128)(2,1)}, bf16[1024,512]{1,0:T(8,128)(2,1)S(1)}, u32[]{:S(2)}) copy-start(bf16[1024,512]{1,0:T(8,128)(2,1)S(1)} %get-tuple-element.15) | copy-start | bytes 3145732
  162.7 4.5 %copy-start.7 = (bf16[1024,512]{1,0:T(8,128)(2,1)}, bf16[1024,512]{1,0:T(8,128)(2,1)S(1)}, u32[]{:S(2)}) copy-start(bf16[1024,512]{1,0:T(8,128)(2,1)S(1)} %get-tuple-element.14) | copy-start | bytes 3145732
  162.7 2.6 %copy-start.2 = (bf16[1,3072,512]{2,1,0:T(8,128)(2,1)S(1)}, bf16[1,3072,512]{2,1,0:T(8,128)(2,1)}, u32[]{:S(2)}) copy-start(bf16[1,3072,512]{2,1,0:T(8,128)(2,1)} %param.10) | copy-start | bytes 9437188
  165.3 1.9 copy-start.4
  169.2 21.5 %collective-permute-start.2 = (bf16[512,3072]{1,0:T(8,128)(2,1)S(1)}, bf16[512,3072]{1,0:T(8,128)(2,1)S(1)}, u32[]{:S(2)}, u32[]{:S(2)}) collective-permute-start(bf16[512,3072]{1,0:T(8,128)(2,1)S(1)} %add_convert_fusion.1), channel_id=1, source_target_pairs={{0,8},{8,0},{1,9},{9,1},{2,10},{10,2},{3,11},{11,3},{4,12},{12,4},... | collective-permute-start | bytes 9437192 | tf_op jit(solution)/shard_map/ppermute | solution.py:51
  169.3 7.6 %collective-permute-start.8 = (f32[8,3072]{1,0:T(8,128)S(1)}, f32[8,3072]{1,0:T(8,128)S(1)}, u32[]{:S(2)}, u32[]{:S(2)}) collective-permute-start(f32[8,3072]{1,0:T(8,128)S(1)} %add_add_fusion.2), channel_id=1, source_target_pairs={{0,3},{1,2},{2,1},{3,0},{4,7},{5,6},{6,5},{7,4},{8,11},{9,10},{10,... | collective-permute-start | bytes 294920 | tf_op jit(solution)/shard_map/ppermute | solution.py:81
  172.1 7.1 %collective-permute-start.7 = (f32[8,3072]{1,0:T(8,128)S(1)}, f32[8,3072]{1,0:T(8,128)S(1)}, u32[]{:S(2)}, u32[]{:S(2)}) collective-permute-start(f32[8,3072]{1,0:T(8,128)S(1)} %add_add_fusion.2), channel_id=1, source_target_pairs={{0,2},{1,3},{2,0},{3,1},{4,6},{5,7},{6,4},{7,5},{8,10},{9,11},{10,... | collective-permute-start | bytes 294920 | tf_op jit(solution)/shard_map/ppermute | solution.py:81
  172.6 6.6 %collective-permute-start.6 = (f32[8,3072]{1,0:T(8,128)S(1)}, f32[8,3072]{1,0:T(8,128)S(1)}, u32[]{:S(2)}, u32[]{:S(2)}) collective-permute-start(f32[8,3072]{1,0:T(8,128)S(1)} %add_add_fusion.2), channel_id=1, source_target_pairs={{0,1},{1,0},{2,3},{3,2},{4,5},{5,4},{6,7},{7,6},{8,9},{9,8},{10,11... | collective-permute-start | bytes 294920 | tf_op jit(solution)/shard_map/ppermute | solution.py:81
  179.2 7.1 %collective-permute-start.11 = (f32[8,3072]{1,0:T(8,128)S(1)}, f32[8,3072]{1,0:T(8,128)S(1)}, u32[]{:S(2)}, u32[]{:S(2)}) collective-permute-start(f32[8,3072]{1,0:T(8,128)S(1)} %add_add_fusion.1), channel_id=1, source_target_pairs={{0,68},{4,64},{64,4},{68,0},{1,69},{5,65},{65,5},{69,1},{2,70},{6,... | collective-permute-start | bytes 294920 | tf_op jit(solution)/shard_map/ppermute | solution.py:81
  181.8 5.1 %collective-permute-start.10 = (f32[8,3072]{1,0:T(8,128)S(1)}, f32[8,3072]{1,0:T(8,128)S(1)}, u32[]{:S(2)}, u32[]{:S(2)}) collective-permute-start(f32[8,3072]{1,0:T(8,128)S(1)} %add_add_fusion.1), channel_id=1, source_target_pairs={{0,64},{4,68},{64,0},{68,4},{1,65},{5,69},{65,1},{69,5},{2,66},{6,... | collective-permute-start | bytes 294920 | tf_op jit(solution)/shard_map/ppermute | solution.py:81
  183.4 6.1 %collective-permute-start.9 = (f32[8,3072]{1,0:T(8,128)S(1)}, f32[8,3072]{1,0:T(8,128)S(1)}, u32[]{:S(2)}, u32[]{:S(2)}) collective-permute-start(f32[8,3072]{1,0:T(8,128)S(1)} %add_add_fusion.1), channel_id=1, source_target_pairs={{0,4},{4,0},{64,68},{68,64},{1,5},{5,1},{65,69},{69,65},{2,6},{6,2... | collective-permute-start | bytes 294920 | tf_op jit(solution)/shard_map/ppermute | solution.py:81
  189.5 4.1 %copy-start.14 = (f32[8,3072]{1,0:T(8,128)}, f32[8,3072]{1,0:T(8,128)S(1)}, u32[]{:S(2)}) copy-start(f32[8,3072]{1,0:T(8,128)S(1)} %add_add_fusion) | copy-start | bytes 294916
  193.6 8.2 %copy-start.10 = (bf16[1024,512]{1,0:T(8,128)(2,1)S(1)}, bf16[1024,512]{1,0:T(8,128)(2,1)}, u32[]{:S(2)}) copy-start(bf16[1024,512]{1,0:T(8,128)(2,1)} %copy-done.9) | copy-start | bytes 3145732
  193.6 48.1 %all-to-all-start.3 = ((bf16[64,8,3072]{2,1,0:T(8,128)(2,1)}), bf16[64,8,3072]{2,1,0:T(8,128)(2,1)}, u32[]{:S(2)}, u32[]{:S(2)}) async-start(bf16[64,8,3072]{2,1,0:T(8,128)(2,1)} %fusion.7), calls=%async_computation.3 | async-start | bytes 6291456 | tf_op jit(solution)/shard_map/all_to_all | solution.py:72
  201.8 7.8 %copy-start.13 = (bf16[8,3072]{1,0:T(8,128)(2,1)S(1)}, bf16[8,3072]{1,0:T(8,128)(2,1)}, u32[]{:S(2)}) copy-start(bf16[8,3072]{1,0:T(8,128)(2,1)} %param.8) | copy-start | bytes 147460
  201.8 7.8 %copy-start.16 = (f32[16]{0:T(128)S(1)}, f32[16]{0:T(128)}, u32[]{:S(2)}) copy-start(f32[16]{0:T(128)} %copy-done.15) | copy-start | bytes 196
  201.8 8.1 %copy-start.8 = (bf16[1024,512]{1,0:T(8,128)(2,1)S(1)}, bf16[1024,512]{1,0:T(8,128)(2,1)}, u32[]{:S(2)}) copy-start(bf16[1024,512]{1,0:T(8,128)(2,1)} %copy-done.7) | copy-start | bytes 3145732
  201.8 16.0 %slice-start = ((s8[6291456]{0:T(1024)(128)(4,1)}), s8[4194304]{0:T(1024)(128)(4,1)S(1)}, s32[]{:S(2)}) async-start(s8[6291456]{0:T(1024)(128)(4,1)} %bitcast.108), calls=%async_computation.6 | async-start | bytes 8388608
  209.9 7.9 %copy-start.6 = (bf16[1024,512]{1,0:T(8,128)(2,1)S(1)}, bf16[1024,512]{1,0:T(8,128)(2,1)}, u32[]{:S(2)}) copy-start(bf16[1024,512]{1,0:T(8,128)(2,1)} %copy-done.5) | copy-start | bytes 3145732
  209.9 7.9 %slice-start.1 = ((s8[6291456]{0:T(1024)(128)(4,1)}), s8[2097152]{0:T(1024)(128)(4,1)S(1)}, s32[]{:S(2)}) async-start(s8[6291456]{0:T(1024)(128)(4,1)} %bitcast.108), calls=%async_computation.7 | async-start | bytes 4194304
  217.9 27.1 %copy-start.1 = (bf16[1,512,3072]{2,1,0:T(8,128)(2,1)S(1)}, bf16[1,512,3072]{2,1,0:T(8,128)(2,1)}, u32[]{:S(2)}) copy-start(bf16[1,512,3072]{2,1,0:T(8,128)(2,1)} %param.12) | copy-start | bytes 9437188
Sparse Core Ops, SparseCore 0:
  25.6 45.1 all-gather.2
  72.5 79.7 all-gather.4

commit v3 on v2

--- a/solution.py
+++ b/solution.py
@@ -78,7 +78,11 @@
 
 def all_sum(part):
     for axis in ("z", "y", ("xl", "xh")):
-        one, two, three = (lax.ppermute(part, axis, flip_perm(4, bit)) for bit in (1, 2, 3))
+        part = lax.reduce_precision(part, 8, 7)
+        rounded = part.astype(BF16)
+        one, two, three = (
+            lax.ppermute(rounded, axis, flip_perm(4, bit)).astype(F32) for bit in (1, 2, 3)
+        )
         part = (part + one) + (two + three)
     return part
 
@@ -124,8 +128,10 @@
         of_core(hidden, 1 - core), down_matrix, preferred_element_type=F32
     ).astype(BF16)
     out_other = swap_cores(out_theirs)
-    out_mine = jnp.dot(of_core(hidden, core), down_matrix, preferred_element_type=F32)
-    out_merged = (out_mine + out_other.astype(F32)).astype(BF16)
+    out_mine = lax.optimization_barrier(
+        jnp.dot(of_core(hidden, core), down_matrix, preferred_element_type=F32).astype(BF16)
+    )
+    out_merged = (out_mine.astype(F32) + out_other.astype(F32)).astype(BF16)
     returned = send_home(out_merged, experts, model_width)
     home = returned
     first_out = contract_rows(first_table.astype(BF16), home)

time: 253 us -> 250 us (0.988)
  waiting for transfers between devices: 54.7 us -> 50.8 us
where the time goes in v3:
time: 250 us; the launch traced here: 249 us
  blocking collectives  83.4 us (33%)
  matrix products  56.8 us (23%)
  waiting for transfers between devices  50.8 us (20%)
  starting transfers between devices  24.7 us (10%)
  between operations  17.7 us (7%)
  other arithmetic  8.12 us (3%)
  local copies, waits for them, and re-layouts  7.77 us (3%)
    all_to_all x1, blocking collectives, send_home(): lax.all_to_all(merged.reshape(8 * experts, CAP, width), EVERY, split_axis...  51.8 us
    all_to_all x2, blocking collectives, exchange(): lax.all_to_all(rows.reshape(experts, CAP, width), OWNERS, split_axis=0, c...  31.7 us
    dot_general x6, matrix products, contract_rows(): lax.dot_general(left_side, right_side, (((0,), (0,)), ((), ())), preferre...  22.7 us
    all_gather x1, waiting for transfers between devices, on_device(): gathered = lax.all_gather(arrived, HOLDERS, axis=0, tiled=True)  22.6 us
    all_to_all x1, waiting for transfers between devices, send_home(): lax.all_to_all(merged.reshape(8 * experts, CAP, width), EVERY, split_axis...  18.5 us
    ppermute x9, starting transfers between devices, all_sum(): lax.ppermute(rounded, axis, flip_perm(4, bit)).astype(F32)  16.9 us
    dot_general x6, matrix products, contract_cols(): lax.dot_general(left_side, right_side, (((1,), (1,)), ((), ())), preferre...  16 us
    all_to_all x1, starting transfers between devices, send_home(): lax.all_to_all(merged.reshape(8 * experts, CAP, width), EVERY, split_axis...  7.21 us
  transfers between devices with their start and end apart: 15, of which 8 were waited for; matrix products, arithmetic and copies ran while one was open for 24% of the time, Pallas kernels for 0%

profile of v3, /device:TPU:24, one launch (start us, length us, event | category | flops | bytes accessed | tf_op | source)
XLA Modules:
  0.0 249.3 jit_solution(18375587428198663483)
XLA Ops:
  7.2 0.0 all-gather.3.cloned.1.call-start
  7.2 0.9 slice_bitcast_fusion.1
  8.1 0.2 convert_reduce_fusion.2
  8.3 0.8 add_add_fusion.2
  9.1 1.2 fusion.5
  10.3 15.1 %all_to_all.20 = bf16[8,8,3072]{2,1,0:T(8,128)(2,1)} all-to-all(bf16[8,8,3072]{2,1,0:T(8,128)(2,1)S(1)} %fusion.5), channel_id=1, replica_groups=mesh['xl'=2,'z'=4,'c'=2,'xh'=2,'y'=4] {'xh','y'}, dimensions={0} | all-to-all | bytes 786432 | tf_op jit(solution)/shard_map/all_to_all | solution.py:60
  25.4 0.0 all-gather.5.cloned.1.call-start
  25.5 1.0 select_reduce_fusion.1
  26.6 0.1 add_reduce_fusion
  26.7 1.2 slice.34
  28.5 1.2 fusion.4
  29.8 16.6 %all_to_all.21 = bf16[8,8,3072]{2,1,0:T(8,128)(2,1)} all-to-all(bf16[8,8,3072]{2,1,0:T(8,128)(2,1)S(1)} %fusion.4), channel_id=1, replica_groups=mesh['xl'=2,'z'=4,'c'=2,'xh'=2,'y'=4] {'xh','y'}, dimensions={0} | all-to-all | bytes 786432 | tf_op jit(solution)/shard_map/all_to_all | solution.py:60
  46.4 1.2 slice.35
  48.2 22.6 %all-gather.3.cloned.1.call-done = bf16[1024,3072]{1,0:T(8,128)(2,1)} async-done(((bf16[64,3072]{1,0:T(8,128)(2,1)}), bf16[1024,3072]{1,0:T(8,128)(2,1)}) %all-gather.3.cloned.1.call-update) | async-done | bytes 6291472 | tf_op jit(solution)/shard_map/all_gather | solution.py:115
  70.8 6.6 %fusion.20 = f32[1024,512]{1,0:T(8,128)S(1)} fusion(bf16[1024,3072]{1,0:T(8,128)(2,1)} %all-gather.3.cloned.1.call-done, bf16[1,3072,512]{2,1,0:T(8,128)(2,1)} %param.10), kind=kOutput, calls=%fused_computation.34 | convolution fusion | flops 3221225472 | bytes 11534336 | tf_op jit(solution)/shard_map/dot_general | solution.py:122
  77.4 4.9 %add_convert_fusion.4 = (bf16[1024,512]{1,0:T(8,128)(2,1)S(1)}, f32[1024,512]{1,0:T(8,128)}) fusion(f32[]{:T(128)} %bitcast.9, f32[1024,512]{1,0:T(8,128)S(1)} %fusion.20, bf16[1024,3072]{1,0:T(8,128)(2,1)S(1)} %copy-done.15, bf16[1,3072,512]{2,1,0:T(8,128)(2,1)S(1)} %copy-done.3), kind=kOutput, calls=%fused_computation.38 | convolution fusion | flops 3224895488 | bytes 14680068 | tf_op jit(solution)/shard_map/dot_general | solution.py:123
  82.3 0.1 constant_dynamic-slice_fusion.5
  82.4 1.8 convolution_convert_fusion.3
  84.2 0.3 collective-permute-start
  84.6 1.8 convolution_convert_fusion.4
  86.4 3.6 %collective-permute-done = bf16[512,3072]{1,0:T(8,128)(2,1)S(1)} collective-permute-done((bf16[512,3072]{1,0:T(8,128)(2,1)S(1)}, bf16[512,3072]{1,0:T(8,128)(2,1)S(1)}, u32[]{:S(2)}, u32[]{:S(2)}) %collective-permute-start) | collective-permute-done | bytes 3145760 | tf_op jit(solution)/shard_map/ppermute | solution.py:51
  90.0 1.2 add_convert_fusion.3
  91.1 51.8 %all_to_all.22 = bf16[64,8,3072]{2,1,0:T(8,128)(2,1)S(1)} all-to-all(bf16[64,8,3072]{2,1,0:T(8,128)(2,1)S(1)} %bitcast.92), channel_id=1, replica_groups=mesh['xl'=2,'z'=4,'c'=2,'xh'=2,'y'=4] {'xl','z','xh','y'}, dimensions={0} | all-to-all | bytes 6291456 | tf_op jit(solution)/shard_map/all_to_all | solution.py:72
  142.9 0.5 bitcast_reduce_fusion.1
  143.4 0.2 fusion.33
  143.7 0.2 copy-done.12
  143.8 1.0 fusion.24
  144.8 0.2 fusion.36
  145.0 0.1 collective-permute-start.1
  145.1 0.5 slice.36
  145.6 0.8 collective-permute-done.1
  146.4 4.2 %collective-permute-start.3 = (bf16[8,3072]{1,0:T(8,128)(2,1)S(1)}, bf16[8,3072]{1,0:T(8,128)(2,1)S(1)}, u32[]{:S(2)}, u32[]{:S(2)}) collective-permute-start(bf16[8,3072]{1,0:T(8,128)(2,1)S(1)} %get-tuple-element.16), channel_id=1, source_target_pairs={{0,16},{16,0},{32,48},{48,32},{1,17},{17,1},{33,49},{49,33},{2,18}... | collective-permute-start | bytes 147464 | tf_op jit(solution)/shard_map/ppermute | solution.py:84
  150.6 1.5 collective-permute-start.4
  152.2 1.2 collective-permute-start.5
  153.4 0.5 slice.37
  155.2 7.7 %multiply_convert_fusion = (bf16[1024,512]{1,0:T(8,128)(2,1)S(1)}, bf16[1024,512]{1,0:T(8,128)(2,1)S(1)}) fusion(f32[]{:T(128)} %bitcast.16, f32[1024,512]{1,0:T(8,128)} %copy-done.16, f32[1024,512]{1,0:T(8,128)} %get-tuple-element.34, bf16[1024,3072]{1,0:T(8,128)(2,1)} %all-gather.5.cloned.1.call-done, bf16[1,512,3072]{2,1,0:T(8,128)(2,1)S(1)} %copy-done), kind=kOutput, calls=%fused_computation.36 | convolution fusion | flops 3228565504 | bytes 15728644 | tf_op jit(solution)/shard_map/dot_general | solution.py:45
  162.9 0.2 constant_dynamic-slice_fusion.2
  163.2 2.4 copy-done.2
  165.6 1.8 fusion.16
  167.4 0.0 copy-done.4
  167.5 1.8 add_convert_fusion.1
  169.3 0.1 collective-permute-start.2
  169.5 0.7 collective-permute-start.6
  170.1 3.5 %collective-permute-start.7 = (bf16[8,3072]{1,0:T(8,128)(2,1)S(1)}, bf16[8,3072]{1,0:T(8,128)(2,1)S(1)}, u32[]{:S(2)}, u32[]{:S(2)}) collective-permute-start(bf16[8,3072]{1,0:T(8,128)(2,1)S(1)} %get-tuple-element.14), channel_id=1, source_target_pairs={{0,2},{1,3},{2,0},{3,1},{4,6},{5,7},{6,4},{7,5},{8,10},{9,11},{10,... | collective-permute-start | bytes 147464 | tf_op jit(solution)/shard_map/ppermute | solution.py:84
  173.6 0.6 collective-permute-start.8
  174.2 1.8 fusion.18
  176.1 0.7 collective-permute-done.7
  176.8 2.1 collective-permute-done.8
  178.9 3.0 %collective-permute-start.10 = (bf16[8,3072]{1,0:T(8,128)(2,1)S(1)}, bf16[8,3072]{1,0:T(8,128)(2,1)S(1)}, u32[]{:S(2)}, u32[]{:S(2)}) collective-permute-start(bf16[8,3072]{1,0:T(8,128)(2,1)S(1)} %fusion.51), channel_id=1, source_target_pairs={{0,64},{4,68},{64,0},{68,4},{1,65},{5,69},{65,1},{69,5},{2,66},{6,... | collective-permute-start | bytes 147464 | tf_op jit(solution)/shard_map/ppermute | solution.py:84
  181.9 0.8 collective-permute-start.11
  182.8 1.3 collective-permute-start.9
  184.1 1.8 add_convert_fusion.2
  186.0 1.3 collective-permute-done.11
  187.3 1.1 collective-permute-done.9
  188.4 0.5 slice.38
  189.6 2.8 %fusion.7 = bf16[64,8,3072]{2,1,0:T(8,128)(2,1)} fusion(bf16[512,3072]{1,0:T(8,128)(2,1)S(1)} %collective-permute-done.2, bf16[512,3072]{1,0:T(8,128)(2,1)S(1)} %add_convert_fusion.2, f32[]{:T(128)} %bitcast.23), kind=kLoop, calls=%fused_computation.19 | loop fusion | flops 7864320 | bytes 9437188 | tf_op jit(solution)/shard_map/reshape | solution.py:73
  192.5 7.2 %all-to-all-start.3 = ((bf16[64,8,3072]{2,1,0:T(8,128)(2,1)}), bf16[64,8,3072]{2,1,0:T(8,128)(2,1)}, u32[]{:S(2)}, u32[]{:S(2)}) async-start(bf16[64,8,3072]{2,1,0:T(8,128)(2,1)} %fusion.7), calls=%async_computation.3 | async-start | bytes 6291456 | tf_op jit(solution)/shard_map/all_to_all | solution.py:72
  199.8 7.8 %fusion.2 = bf16[1,512,3072]{2,1,0:T(8,128)(2,1)} fusion(bf16[1024,512]{1,0:T(8,128)(2,1)S(1)} %copy-done.10, bf16[1024,3072]{1,0:T(8,128)(2,1)} %all-gather.5.cloned.1.call-done), kind=kOutput, calls=%fused_computation.11 | convolution fusion | flops 3222798336 | bytes 10485760 | tf_op jit(solution)/shard_map/dot_general | solution.py:39
  207.5 0.3 fusion.35
  207.9 7.9 %fusion = bf16[1,3072,512]{2,1,0:T(8,128)(2,1)} fusion(bf16[1024,3072]{1,0:T(8,128)(2,1)} %all-gather.3.cloned.1.call-done, bf16[1024,512]{1,0:T(8,128)(2,1)S(1)} %copy-done.8), kind=kOutput, calls=%fused_computation.9 | convolution fusion | flops 3222798336 | bytes 10485760 | tf_op jit(solution)/shard_map/dot_general | solution.py:39
  215.8 4.9 %fusion.1 = bf16[1,3072,512]{2,1,0:T(8,128)(2,1)} fusion(bf16[1024,3072]{1,0:T(8,128)(2,1)S(1)} %bitcast.107, bf16[1024,512]{1,0:T(8,128)(2,1)S(1)} %copy-done.6), kind=kOutput, calls=%fused_computation.10 | convolution fusion | flops 3222798336 | bytes 10485760 | tf_op jit(solution)/shard_map/dot_general | solution.py:39
  220.7 18.5 %all-to-all-done.3 = bf16[64,8,3072]{2,1,0:T(8,128)(2,1)} async-done(((bf16[64,8,3072]{2,1,0:T(8,128)(2,1)}), bf16[64,8,3072]{2,1,0:T(8,128)(2,1)}, u32[]{:S(2)}, u32[]{:S(2)}) %all-to-all-start.3) | async-done | bytes 3145760 | tf_op jit(solution)/shard_map/all_to_all | solution.py:72
  239.2 2.4 bitcast_reduce_fusion
  241.6 0.9 fusion.6
  (52 shorter events, 0.3 us)
Async XLA Ops:
  7.2 75.2 %copy-start = (bf16[1,512,3072]{2,1,0:T(8,128)(2,1)S(1)}, bf16[1,512,3072]{2,1,0:T(8,128)(2,1)}, u32[]{:S(2)}) copy-start(bf16[1,512,3072]{2,1,0:T(8,128)(2,1)} %param.12) | copy-start | bytes 9437188
  7.2 63.6 %all-gather.3.cloned.1.call-start = ((), (), s32[]{:S(2)}) async-start(), calls=%async_computation.4 | async-start | bytes 6684672 | tf_op jit(solution)/shard_map/all_gather | solution.py:115
  25.4 129.8 %all-gather.5.cloned.1.call-start = ((), (), s32[]{:S(2)}) async-start(), calls=%async_computation.5 | async-start | bytes 6684672 | tf_op jit(solution)/shard_map/all_gather | solution.py:116
  70.8 6.6 %copy-start.3 = (bf16[1,3072,512]{2,1,0:T(8,128)(2,1)S(1)}, bf16[1,3072,512]{2,1,0:T(8,128)(2,1)}, u32[]{:S(2)}) copy-start(bf16[1,3072,512]{2,1,0:T(8,128)(2,1)} %param.11) | copy-start | bytes 9437188
  70.8 6.6 %copy-start.15 = (bf16[1024,3072]{1,0:T(8,128)(2,1)S(1)}, bf16[1024,3072]{1,0:T(8,128)(2,1)}, u32[]{:S(2)}) copy-start(bf16[1024,3072]{1,0:T(8,128)(2,1)} %all-gather.3.cloned.1.call-done) | copy-start | bytes 18874372
  77.4 5.0 %copy-start.16 = (f32[1024,512]{1,0:T(8,128)}, f32[1024,512]{1,0:T(8,128)S(1)}, u32[]{:S(2)}) copy-start(f32[1024,512]{1,0:T(8,128)S(1)} %fusion.20) | copy-start | bytes 6291460
  82.3 1.9 copy-start.9
  84.2 5.7 %collective-permute-start = (bf16[512,3072]{1,0:T(8,128)(2,1)S(1)}, bf16[512,3072]{1,0:T(8,128)(2,1)S(1)}, u32[]{:S(2)}, u32[]{:S(2)}) collective-permute-start(bf16[512,3072]{1,0:T(8,128)(2,1)S(1)} %convolution_convert_fusion.3), channel_id=1, source_target_pairs={{0,8},{8,0},{1,9},{9,1},{2,10},{10,2},{3,11},{11,3},{4,12},{12,4},... | collective-permute-start | bytes 9437192 | tf_op jit(solution)/shard_map/ppermute | solution.py:51
  142.9 0.9 copy-start.12
  142.9 1.9 copy-start.11
  145.0 1.4 collective-permute-start.1
  146.4 23.0 %collective-permute-start.3 = (bf16[8,3072]{1,0:T(8,128)(2,1)S(1)}, bf16[8,3072]{1,0:T(8,128)(2,1)S(1)}, u32[]{:S(2)}, u32[]{:S(2)}) collective-permute-start(bf16[8,3072]{1,0:T(8,128)(2,1)S(1)} %get-tuple-element.16), channel_id=1, source_target_pairs={{0,16},{16,0},{32,48},{48,32},{1,17},{17,1},{33,49},{49,33},{2,18}... | collective-permute-start | bytes 147464 | tf_op jit(solution)/shard_map/ppermute | solution.py:84
  150.6 18.8 %collective-permute-start.4 = (bf16[8,3072]{1,0:T(8,128)(2,1)S(1)}, bf16[8,3072]{1,0:T(8,128)(2,1)S(1)}, u32[]{:S(2)}, u32[]{:S(2)}) collective-permute-start(bf16[8,3072]{1,0:T(8,128)(2,1)S(1)} %get-tuple-element.16), channel_id=1, source_target_pairs={{0,32},{16,48},{32,0},{48,16},{1,33},{17,49},{33,1},{49,17},{2,34}... | collective-permute-start | bytes 147464 | tf_op jit(solution)/shard_map/ppermute | solution.py:84
  152.2 17.2 %collective-permute-start.5 = (bf16[8,3072]{1,0:T(8,128)(2,1)S(1)}, bf16[8,3072]{1,0:T(8,128)(2,1)S(1)}, u32[]{:S(2)}, u32[]{:S(2)}) collective-permute-start(bf16[8,3072]{1,0:T(8,128)(2,1)S(1)} %get-tuple-element.16), channel_id=1, source_target_pairs={{0,48},{16,32},{32,16},{48,0},{1,49},{17,33},{33,17},{49,1},{2,50}... | collective-permute-start | bytes 147464 | tf_op jit(solution)/shard_map/ppermute | solution.py:84
  162.9 4.5 %copy-start.5 = (bf16[1024,512]{1,0:T(8,128)(2,1)}, bf16[1024,512]{1,0:T(8,128)(2,1)S(1)}, u32[]{:S(2)}) copy-start(bf16[1024,512]{1,0:T(8,128)(2,1)S(1)} %get-tuple-element.18) | copy-start | bytes 3145732
  162.9 4.5 %copy-start.7 = (bf16[1024,512]{1,0:T(8,128)(2,1)}, bf16[1024,512]{1,0:T(8,128)(2,1)S(1)}, u32[]{:S(2)}) copy-start(bf16[1024,512]{1,0:T(8,128)(2,1)S(1)} %get-tuple-element.19) | copy-start | bytes 3145732
  162.9 2.6 %copy-start.2 = (bf16[1,3072,512]{2,1,0:T(8,128)(2,1)S(1)}, bf16[1,3072,512]{2,1,0:T(8,128)(2,1)}, u32[]{:S(2)}) copy-start(bf16[1,3072,512]{2,1,0:T(8,128)(2,1)} %param.10) | copy-start | bytes 9437188
  165.6 1.9 copy-start.4
  169.3 20.3 %collective-permute-start.2 = (bf16[512,3072]{1,0:T(8,128)(2,1)S(1)}, bf16[512,3072]{1,0:T(8,128)(2,1)S(1)}, u32[]{:S(2)}, u32[]{:S(2)}) collective-permute-start(bf16[512,3072]{1,0:T(8,128)(2,1)S(1)} %add_convert_fusion.1), channel_id=1, source_target_pairs={{0,8},{8,0},{1,9},{9,1},{2,10},{10,2},{3,11},{11,3},{4,12},{12,4},... | collective-permute-start | bytes 9437192 | tf_op jit(solution)/shard_map/ppermute | solution.py:51
  169.5 6.6 %collective-permute-start.6 = (bf16[8,3072]{1,0:T(8,128)(2,1)S(1)}, bf16[8,3072]{1,0:T(8,128)(2,1)S(1)}, u32[]{:S(2)}, u32[]{:S(2)}) collective-permute-start(bf16[8,3072]{1,0:T(8,128)(2,1)S(1)} %get-tuple-element.14), channel_id=1, source_target_pairs={{0,1},{1,0},{2,3},{3,2},{4,5},{5,4},{6,7},{7,6},{8,9},{9,8},{10,11... | collective-permute-start | bytes 147464 | tf_op jit(solution)/shard_map/ppermute | solution.py:84
  170.1 6.6 %collective-permute-start.7 = (bf16[8,3072]{1,0:T(8,128)(2,1)S(1)}, bf16[8,3072]{1,0:T(8,128)(2,1)S(1)}, u32[]{:S(2)}, u32[]{:S(2)}) collective-permute-start(bf16[8,3072]{1,0:T(8,128)(2,1)S(1)} %get-tuple-element.14), channel_id=1, source_target_pairs={{0,2},{1,3},{2,0},{3,1},{4,6},{5,7},{6,4},{7,5},{8,10},{9,11},{10,... | collective-permute-start | bytes 147464 | tf_op jit(solution)/shard_map/ppermute | solution.py:84
  173.6 5.3 %collective-permute-start.8 = (bf16[8,3072]{1,0:T(8,128)(2,1)S(1)}, bf16[8,3072]{1,0:T(8,128)(2,1)S(1)}, u32[]{:S(2)}, u32[]{:S(2)}) collective-permute-start(bf16[8,3072]{1,0:T(8,128)(2,1)S(1)} %get-tuple-element.14), channel_id=1, source_target_pairs={{0,3},{1,2},{2,1},{3,0},{4,7},{5,6},{6,5},{7,4},{8,11},{9,10},{10,... | collective-permute-start | bytes 147464 | tf_op jit(solution)/shard_map/ppermute | solution.py:84
  178.9 7.0 %collective-permute-start.10 = (bf16[8,3072]{1,0:T(8,128)(2,1)S(1)}, bf16[8,3072]{1,0:T(8,128)(2,1)S(1)}, u32[]{:S(2)}, u32[]{:S(2)}) collective-permute-start(bf16[8,3072]{1,0:T(8,128)(2,1)S(1)} %fusion.51), channel_id=1, source_target_pairs={{0,64},{4,68},{64,0},{68,4},{1,65},{5,69},{65,1},{69,5},{2,66},{6,... | collective-permute-start | bytes 147464 | tf_op jit(solution)/shard_map/ppermute | solution.py:84
  181.9 5.3 %collective-permute-start.11 = (bf16[8,3072]{1,0:T(8,128)(2,1)S(1)}, bf16[8,3072]{1,0:T(8,128)(2,1)S(1)}, u32[]{:S(2)}, u32[]{:S(2)}) collective-permute-start(bf16[8,3072]{1,0:T(8,128)(2,1)S(1)} %fusion.51), channel_id=1, source_target_pairs={{0,68},{4,64},{64,4},{68,0},{1,69},{5,65},{65,5},{69,1},{2,70},{6,... | collective-permute-start | bytes 147464 | tf_op jit(solution)/shard_map/ppermute | solution.py:84
  182.8 5.6 %collective-permute-start.9 = (bf16[8,3072]{1,0:T(8,128)(2,1)S(1)}, bf16[8,3072]{1,0:T(8,128)(2,1)S(1)}, u32[]{:S(2)}, u32[]{:S(2)}) collective-permute-start(bf16[8,3072]{1,0:T(8,128)(2,1)S(1)} %fusion.51), channel_id=1, source_target_pairs={{0,4},{4,0},{64,68},{68,64},{1,5},{5,1},{65,69},{69,65},{2,6},{6,2... | collective-permute-start | bytes 147464 | tf_op jit(solution)/shard_map/ppermute | solution.py:84
  188.4 4.1 %copy-start.14 = (f32[8,3072]{1,0:T(8,128)}, f32[8,3072]{1,0:T(8,128)S(1)}, u32[]{:S(2)}) copy-start(f32[8,3072]{1,0:T(8,128)S(1)} %add_add_fusion) | copy-start | bytes 294916
  192.5 7.2 %copy-start.10 = (bf16[1024,512]{1,0:T(8,128)(2,1)S(1)}, bf16[1024,512]{1,0:T(8,128)(2,1)}, u32[]{:S(2)}) copy-start(bf16[1024,512]{1,0:T(8,128)(2,1)} %copy-done.9) | copy-start | bytes 3145732
  192.5 46.7 %all-to-all-start.3 = ((bf16[64,8,3072]{2,1,0:T(8,128)(2,1)}), bf16[64,8,3072]{2,1,0:T(8,128)(2,1)}, u32[]{:S(2)}, u32[]{:S(2)}) async-start(bf16[64,8,3072]{2,1,0:T(8,128)(2,1)} %fusion.7), calls=%async_computation.3 | async-start | bytes 6291456 | tf_op jit(solution)/shard_map/all_to_all | solution.py:72
  199.7 7.8 %copy-start.13 = (bf16[8,3072]{1,0:T(8,128)(2,1)S(1)}, bf16[8,3072]{1,0:T(8,128)(2,1)}, u32[]{:S(2)}) copy-start(bf16[8,3072]{1,0:T(8,128)(2,1)} %param.8) | copy-start | bytes 147460
  199.7 8.1 %copy-start.8 = (bf16[1024,512]{1,0:T(8,128)(2,1)S(1)}, bf16[1024,512]{1,0:T(8,128)(2,1)}, u32[]{:S(2)}) copy-start(bf16[1024,512]{1,0:T(8,128)(2,1)} %copy-done.7) | copy-start | bytes 3145732
  199.7 16.0 %slice-start = ((s8[6291456]{0:T(1024)(128)(4,1)}), s8[4194304]{0:T(1024)(128)(4,1)S(1)}, s32[]{:S(2)}) async-start(s8[6291456]{0:T(1024)(128)(4,1)} %bitcast.106), calls=%async_computation.6 | async-start | bytes 8388608
  207.8 7.9 %copy-start.6 = (bf16[1024,512]{1,0:T(8,128)(2,1)S(1)}, bf16[1024,512]{1,0:T(8,128)(2,1)}, u32[]{:S(2)}) copy-start(bf16[1024,512]{1,0:T(8,128)(2,1)} %copy-done.5) | copy-start | bytes 3145732
  207.9 7.9 %slice-start.1 = ((s8[6291456]{0:T(1024)(128)(4,1)}), s8[2097152]{0:T(1024)(128)(4,1)S(1)}, s32[]{:S(2)}) async-start(s8[6291456]{0:T(1024)(128)(4,1)} %bitcast.106), calls=%async_computation.7 | async-start | bytes 4194304
  215.8 26.7 %copy-start.1 = (bf16[1,512,3072]{2,1,0:T(8,128)(2,1)S(1)}, bf16[1,512,3072]{2,1,0:T(8,128)(2,1)}, u32[]{:S(2)}) copy-start(bf16[1,512,3072]{2,1,0:T(8,128)(2,1)} %param.12) | copy-start | bytes 9437188
Sparse Core Ops, SparseCore 0:
  25.6 45.1 all-gather.2
  72.5 79.5 all-gather.4

commit v4 on v3

--- a/solution.py
+++ b/solution.py
@@ -158,8 +158,8 @@
     gate_grad = (hidden_grad * pre_up * silu_slope).astype(BF16)
 
     def back(which):
-        return contract_cols(of_core(gate_grad, which), gate_matrix) + contract_cols(
-            of_core(up_grad, which), up_matrix
+        return contract_cols(of_core(up_grad, which), up_matrix) + contract_cols(
+            of_core(gate_grad, which), gate_matrix
         )
 
     back_other = swap_cores(back(1 - core).astype(BF16))

time: 250 us -> 250 us (level)
  no operation moved by 1% of the time
where the time goes in v4:
time: 250 us; the launch traced here: 249 us
  blocking collectives  83.4 us (33%)
  matrix products  56.7 us (23%)
  waiting for transfers between devices  50.8 us (20%)
  starting transfers between devices  24.7 us (10%)
  between operations  17.7 us (7%)
  other arithmetic  8.12 us (3%)
  local copies, waits for them, and re-layouts  7.77 us (3%)
    all_to_all x1, blocking collectives, send_home(): lax.all_to_all(merged.reshape(8 * experts, CAP, width), EVERY, split_axis...  51.8 us
    all_to_all x2, blocking collectives, exchange(): lax.all_to_all(rows.reshape(experts, CAP, width), OWNERS, split_axis=0, c...  31.7 us
    dot_general x6, matrix products, contract_rows(): lax.dot_general(left_side, right_side, (((0,), (0,)), ((), ())), preferre...  22.7 us
    all_gather x1, waiting for transfers between devices, on_device(): gathered = lax.all_gather(arrived, HOLDERS, axis=0, tiled=True)  22.6 us
    all_to_all x1, waiting for transfers between devices, send_home(): lax.all_to_all(merged.reshape(8 * experts, CAP, width), EVERY, split_axis...  18.5 us
    ppermute x9, starting transfers between devices, all_sum(): lax.ppermute(rounded, axis, flip_perm(4, bit)).astype(F32)  16.9 us
    dot_general x6, matrix products, contract_cols(): lax.dot_general(left_side, right_side, (((1,), (1,)), ((), ())), preferre...  16 us
    all_to_all x1, starting transfers between devices, send_home(): lax.all_to_all(merged.reshape(8 * experts, CAP, width), EVERY, split_axis...  7.21 us
  transfers between devices with their start and end apart: 15, of which 8 were waited for; matrix products, arithmetic and copies ran while one was open for 24% of the time, Pallas kernels for 0%

profile of v4, /device:TPU:24, one launch (start us, length us, event | category | flops | bytes accessed | tf_op | source)
XLA Modules:
  0.0 249.3 jit_solution(17816416163336003792)
XLA Ops:
  7.2 0.0 all-gather.3.cloned.1.call-start
  7.2 0.9 slice_bitcast_fusion.1
  8.1 0.2 convert_reduce_fusion.2
  8.3 0.8 add_add_fusion.2
  9.1 1.2 fusion.5
  10.3 15.1 %all_to_all.20 = bf16[8,8,3072]{2,1,0:T(8,128)(2,1)} all-to-all(bf16[8,8,3072]{2,1,0:T(8,128)(2,1)S(1)} %fusion.5), channel_id=1, replica_groups=mesh['xl'=2,'z'=4,'c'=2,'xh'=2,'y'=4] {'xh','y'}, dimensions={0} | all-to-all | bytes 786432 | tf_op jit(solution)/shard_map/all_to_all | solution.py:60
  25.4 0.0 all-gather.5.cloned.1.call-start
  25.5 1.0 select_reduce_fusion.1
  26.6 0.1 add_reduce_fusion
  26.7 1.2 slice.34
  28.5 1.2 fusion.4
  29.8 16.6 %all_to_all.21 = bf16[8,8,3072]{2,1,0:T(8,128)(2,1)} all-to-all(bf16[8,8,3072]{2,1,0:T(8,128)(2,1)S(1)} %fusion.4), channel_id=1, replica_groups=mesh['xl'=2,'z'=4,'c'=2,'xh'=2,'y'=4] {'xh','y'}, dimensions={0} | all-to-all | bytes 786432 | tf_op jit(solution)/shard_map/all_to_all | solution.py:60
  46.4 1.2 slice.35
  48.2 22.6 %all-gather.3.cloned.1.call-done = bf16[1024,3072]{1,0:T(8,128)(2,1)} async-done(((bf16[64,3072]{1,0:T(8,128)(2,1)}), bf16[1024,3072]{1,0:T(8,128)(2,1)}) %all-gather.3.cloned.1.call-update) | async-done | bytes 6291472 | tf_op jit(solution)/shard_map/all_gather | solution.py:115
  70.8 6.6 %fusion.20 = f32[1024,512]{1,0:T(8,128)S(1)} fusion(bf16[1024,3072]{1,0:T(8,128)(2,1)} %all-gather.3.cloned.1.call-done, bf16[1,3072,512]{2,1,0:T(8,128)(2,1)} %param.10), kind=kOutput, calls=%fused_computation.34 | convolution fusion | flops 3221225472 | bytes 11534336 | tf_op jit(solution)/shard_map/dot_general | solution.py:122
  77.4 4.9 %add_convert_fusion.4 = (bf16[1024,512]{1,0:T(8,128)(2,1)S(1)}, f32[1024,512]{1,0:T(8,128)}) fusion(f32[]{:T(128)} %bitcast.9, f32[1024,512]{1,0:T(8,128)S(1)} %fusion.20, bf16[1024,3072]{1,0:T(8,128)(2,1)S(1)} %copy-done.15, bf16[1,3072,512]{2,1,0:T(8,128)(2,1)S(1)} %copy-done.2), kind=kOutput, calls=%fused_computation.38 | convolution fusion | flops 3224895488 | bytes 14680068 | tf_op jit(solution)/shard_map/dot_general | solution.py:123
  82.3 0.1 constant_dynamic-slice_fusion.5
  82.4 1.8 convolution_convert_fusion.3
  84.2 0.3 collective-permute-start
  84.6 1.8 convolution_convert_fusion.4
  86.4 3.6 %collective-permute-done = bf16[512,3072]{1,0:T(8,128)(2,1)S(1)} collective-permute-done((bf16[512,3072]{1,0:T(8,128)(2,1)S(1)}, bf16[512,3072]{1,0:T(8,128)(2,1)S(1)}, u32[]{:S(2)}, u32[]{:S(2)}) %collective-permute-start) | collective-permute-done | bytes 3145760 | tf_op jit(solution)/shard_map/ppermute | solution.py:51
  90.0 1.2 add_convert_fusion.3
  91.1 51.8 %all_to_all.22 = bf16[64,8,3072]{2,1,0:T(8,128)(2,1)S(1)} all-to-all(bf16[64,8,3072]{2,1,0:T(8,128)(2,1)S(1)} %bitcast.92), channel_id=1, replica_groups=mesh['xl'=2,'z'=4,'c'=2,'xh'=2,'y'=4] {'xl','z','xh','y'}, dimensions={0} | all-to-all | bytes 6291456 | tf_op jit(solution)/shard_map/all_to_all | solution.py:72
  142.9 0.5 bitcast_reduce_fusion.1
  143.4 0.2 fusion.33
  143.7 0.2 copy-done.12
  143.8 1.0 fusion.24
  144.8 0.2 fusion.36
  145.0 0.1 collective-permute-start.1
  145.1 0.5 slice.36
  145.6 0.8 collective-permute-done.1
  146.4 4.2 %collective-permute-start.3 = (bf16[8,3072]{1,0:T(8,128)(2,1)S(1)}, bf16[8,3072]{1,0:T(8,128)(2,1)S(1)}, u32[]{:S(2)}, u32[]{:S(2)}) collective-permute-start(bf16[8,3072]{1,0:T(8,128)(2,1)S(1)} %get-tuple-element.16), channel_id=1, source_target_pairs={{0,16},{16,0},{32,48},{48,32},{1,17},{17,1},{33,49},{49,33},{2,18}... | collective-permute-start | bytes 147464 | tf_op jit(solution)/shard_map/ppermute | solution.py:84
  150.6 1.5 collective-permute-start.4
  152.2 1.2 collective-permute-start.5
  153.4 0.5 slice.37
  155.2 7.6 %multiply_convert_fusion = (bf16[1024,512]{1,0:T(8,128)(2,1)S(1)}, bf16[1024,512]{1,0:T(8,128)(2,1)S(1)}) fusion(f32[1024,512]{1,0:T(8,128)} %copy-done.16, f32[1024,512]{1,0:T(8,128)} %get-tuple-element.34, f32[]{:T(128)} %bitcast.16, bf16[1024,3072]{1,0:T(8,128)(2,1)} %all-gather.5.cloned.1.call-done, bf16[1,512,3072]{2,1,0:T(8,128)(2,1)S(1)} %copy-done), kind=kOutput, calls=%fused_computation.36 | convolution fusion | flops 3228565504 | bytes 15728644 | tf_op jit(solution)/shard_map/dot_general | solution.py:45
  162.9 0.2 constant_dynamic-slice_fusion.2
  163.1 2.4 copy-done.3
  165.5 1.8 fusion.12
  167.4 0.0 copy-done.4
  167.4 1.8 add_convert_fusion.1
  169.3 0.1 collective-permute-start.2
  169.4 0.7 collective-permute-start.6
  170.1 3.5 %collective-permute-start.7 = (bf16[8,3072]{1,0:T(8,128)(2,1)S(1)}, bf16[8,3072]{1,0:T(8,128)(2,1)S(1)}, u32[]{:S(2)}, u32[]{:S(2)}) collective-permute-start(bf16[8,3072]{1,0:T(8,128)(2,1)S(1)} %get-tuple-element.14), channel_id=1, source_target_pairs={{0,2},{1,3},{2,0},{3,1},{4,6},{5,7},{6,4},{7,5},{8,10},{9,11},{10,... | collective-permute-start | bytes 147464 | tf_op jit(solution)/shard_map/ppermute | solution.py:84
  173.6 0.6 collective-permute-start.8
  174.2 1.8 fusion.14
  176.1 0.7 collective-permute-done.7
  176.7 2.1 collective-permute-done.8
  178.9 3.0 %collective-permute-start.10 = (bf16[8,3072]{1,0:T(8,128)(2,1)S(1)}, bf16[8,3072]{1,0:T(8,128)(2,1)S(1)}, u32[]{:S(2)}, u32[]{:S(2)}) collective-permute-start(bf16[8,3072]{1,0:T(8,128)(2,1)S(1)} %fusion.51), channel_id=1, source_target_pairs={{0,64},{4,68},{64,0},{68,4},{1,65},{5,69},{65,1},{69,5},{2,66},{6,... | collective-permute-start | bytes 147464 | tf_op jit(solution)/shard_map/ppermute | solution.py:84
  181.9 0.8 collective-permute-start.11
  182.8 1.3 collective-permute-start.9
  184.1 1.8 add_convert_fusion.2
  185.9 1.3 collective-permute-done.11
  187.2 1.1 collective-permute-done.9
  188.4 0.5 slice.38
  189.6 2.8 %fusion.7 = bf16[64,8,3072]{2,1,0:T(8,128)(2,1)} fusion(bf16[512,3072]{1,0:T(8,128)(2,1)S(1)} %collective-permute-done.2, bf16[512,3072]{1,0:T(8,128)(2,1)S(1)} %add_convert_fusion.2, f32[]{:T(128)} %bitcast.23), kind=kLoop, calls=%fused_computation.19 | loop fusion | flops 7864320 | bytes 9437188 | tf_op jit(solution)/shard_map/reshape | solution.py:73
  192.5 7.2 %all-to-all-start.3 = ((bf16[64,8,3072]{2,1,0:T(8,128)(2,1)}), bf16[64,8,3072]{2,1,0:T(8,128)(2,1)}, u32[]{:S(2)}, u32[]{:S(2)}) async-start(bf16[64,8,3072]{2,1,0:T(8,128)(2,1)} %fusion.7), calls=%async_computation.3 | async-start | bytes 6291456 | tf_op jit(solution)/shard_map/all_to_all | solution.py:72
  199.7 7.8 %fusion.2 = bf16[1,512,3072]{2,1,0:T(8,128)(2,1)} fusion(bf16[1024,512]{1,0:T(8,128)(2,1)S(1)} %copy-done.10, bf16[1024,3072]{1,0:T(8,128)(2,1)} %all-gather.5.cloned.1.call-done), kind=kOutput, calls=%fused_computation.11 | convolution fusion | flops 3222798336 | bytes 10485760 | tf_op jit(solution)/shard_map/dot_general | solution.py:39
  207.5 0.3 fusion.35
  207.8 7.9 %fusion = bf16[1,3072,512]{2,1,0:T(8,128)(2,1)} fusion(bf16[1024,3072]{1,0:T(8,128)(2,1)} %all-gather.3.cloned.1.call-done, bf16[1024,512]{1,0:T(8,128)(2,1)S(1)} %copy-done.8), kind=kOutput, calls=%fused_computation.9 | convolution fusion | flops 3222798336 | bytes 10485760 | tf_op jit(solution)/shard_map/dot_general | solution.py:39
  215.8 4.9 %fusion.1 = bf16[1,3072,512]{2,1,0:T(8,128)(2,1)} fusion(bf16[1024,3072]{1,0:T(8,128)(2,1)S(1)} %bitcast.107, bf16[1024,512]{1,0:T(8,128)(2,1)S(1)} %copy-done.6), kind=kOutput, calls=%fused_computation.10 | convolution fusion | flops 3222798336 | bytes 10485760 | tf_op jit(solution)/shard_map/dot_general | solution.py:39
  220.7 18.5 %all-to-all-done.3 = bf16[64,8,3072]{2,1,0:T(8,128)(2,1)} async-done(((bf16[64,8,3072]{2,1,0:T(8,128)(2,1)}), bf16[64,8,3072]{2,1,0:T(8,128)(2,1)}, u32[]{:S(2)}, u32[]{:S(2)}) %all-to-all-start.3) | async-done | bytes 3145760 | tf_op jit(solution)/shard_map/all_to_all | solution.py:72
  239.2 2.4 bitcast_reduce_fusion
  241.6 0.9 fusion.6
  (52 shorter events, 0.3 us)
Async XLA Ops:
  7.2 75.2 %copy-start = (bf16[1,512,3072]{2,1,0:T(8,128)(2,1)S(1)}, bf16[1,512,3072]{2,1,0:T(8,128)(2,1)}, u32[]{:S(2)}) copy-start(bf16[1,512,3072]{2,1,0:T(8,128)(2,1)} %param.12) | copy-start | bytes 9437188
  7.2 63.6 %all-gather.3.cloned.1.call-start = ((), (), s32[]{:S(2)}) async-start(), calls=%async_computation.4 | async-start | bytes 6684672 | tf_op jit(solution)/shard_map/all_gather | solution.py:115
  25.4 129.8 %all-gather.5.cloned.1.call-start = ((), (), s32[]{:S(2)}) async-start(), calls=%async_computation.5 | async-start | bytes 6684672 | tf_op jit(solution)/shard_map/all_gather | solution.py:116
  70.8 6.6 %copy-start.2 = (bf16[1,3072,512]{2,1,0:T(8,128)(2,1)S(1)}, bf16[1,3072,512]{2,1,0:T(8,128)(2,1)}, u32[]{:S(2)}) copy-start(bf16[1,3072,512]{2,1,0:T(8,128)(2,1)} %param.11) | copy-start | bytes 9437188
  70.8 6.6 %copy-start.15 = (bf16[1024,3072]{1,0:T(8,128)(2,1)S(1)}, bf16[1024,3072]{1,0:T(8,128)(2,1)}, u32[]{:S(2)}) copy-start(bf16[1024,3072]{1,0:T(8,128)(2,1)} %all-gather.3.cloned.1.call-done) | copy-start | bytes 18874372
  77.4 5.0 %copy-start.16 = (f32[1024,512]{1,0:T(8,128)}, f32[1024,512]{1,0:T(8,128)S(1)}, u32[]{:S(2)}) copy-start(f32[1024,512]{1,0:T(8,128)S(1)} %fusion.20) | copy-start | bytes 6291460
  82.3 1.9 copy-start.9
  84.2 5.7 %collective-permute-start = (bf16[512,3072]{1,0:T(8,128)(2,1)S(1)}, bf16[512,3072]{1,0:T(8,128)(2,1)S(1)}, u32[]{:S(2)}, u32[]{:S(2)}) collective-permute-start(bf16[512,3072]{1,0:T(8,128)(2,1)S(1)} %convolution_convert_fusion.3), channel_id=1, source_target_pairs={{0,8},{8,0},{1,9},{9,1},{2,10},{10,2},{3,11},{11,3},{4,12},{12,4},... | collective-permute-start | bytes 9437192 | tf_op jit(solution)/shard_map/ppermute | solution.py:51
  142.9 0.9 copy-start.12
  142.9 1.9 copy-start.11
  145.0 1.4 collective-permute-start.1
  146.4 23.0 %collective-permute-start.3 = (bf16[8,3072]{1,0:T(8,128)(2,1)S(1)}, bf16[8,3072]{1,0:T(8,128)(2,1)S(1)}, u32[]{:S(2)}, u32[]{:S(2)}) collective-permute-start(bf16[8,3072]{1,0:T(8,128)(2,1)S(1)} %get-tuple-element.16), channel_id=1, source_target_pairs={{0,16},{16,0},{32,48},{48,32},{1,17},{17,1},{33,49},{49,33},{2,18}... | collective-permute-start | bytes 147464 | tf_op jit(solution)/shard_map/ppermute | solution.py:84
  150.6 18.7 %collective-permute-start.4 = (bf16[8,3072]{1,0:T(8,128)(2,1)S(1)}, bf16[8,3072]{1,0:T(8,128)(2,1)S(1)}, u32[]{:S(2)}, u32[]{:S(2)}) collective-permute-start(bf16[8,3072]{1,0:T(8,128)(2,1)S(1)} %get-tuple-element.16), channel_id=1, source_target_pairs={{0,32},{16,48},{32,0},{48,16},{1,33},{17,49},{33,1},{49,17},{2,34}... | collective-permute-start | bytes 147464 | tf_op jit(solution)/shard_map/ppermute | solution.py:84
  152.2 17.2 %collective-permute-start.5 = (bf16[8,3072]{1,0:T(8,128)(2,1)S(1)}, bf16[8,3072]{1,0:T(8,128)(2,1)S(1)}, u32[]{:S(2)}, u32[]{:S(2)}) collective-permute-start(bf16[8,3072]{1,0:T(8,128)(2,1)S(1)} %get-tuple-element.16), channel_id=1, source_target_pairs={{0,48},{16,32},{32,16},{48,0},{1,49},{17,33},{33,17},{49,1},{2,50}... | collective-permute-start | bytes 147464 | tf_op jit(solution)/shard_map/ppermute | solution.py:84
  162.9 4.5 %copy-start.5 = (bf16[1024,512]{1,0:T(8,128)(2,1)}, bf16[1024,512]{1,0:T(8,128)(2,1)S(1)}, u32[]{:S(2)}) copy-start(bf16[1024,512]{1,0:T(8,128)(2,1)S(1)} %get-tuple-element.19) | copy-start | bytes 3145732
  162.9 4.5 %copy-start.7 = (bf16[1024,512]{1,0:T(8,128)(2,1)}, bf16[1024,512]{1,0:T(8,128)(2,1)S(1)}, u32[]{:S(2)}) copy-start(bf16[1024,512]{1,0:T(8,128)(2,1)S(1)} %get-tuple-element.18) | copy-start | bytes 3145732
  162.9 2.6 %copy-start.3 = (bf16[1,3072,512]{2,1,0:T(8,128)(2,1)S(1)}, bf16[1,3072,512]{2,1,0:T(8,128)(2,1)}, u32[]{:S(2)}) copy-start(bf16[1,3072,512]{2,1,0:T(8,128)(2,1)} %param.11) | copy-start | bytes 9437188
  165.5 1.9 copy-start.4
  169.3 20.3 %collective-permute-start.2 = (bf16[512,3072]{1,0:T(8,128)(2,1)S(1)}, bf16[512,3072]{1,0:T(8,128)(2,1)S(1)}, u32[]{:S(2)}, u32[]{:S(2)}) collective-permute-start(bf16[512,3072]{1,0:T(8,128)(2,1)S(1)} %add_convert_fusion.1), channel_id=1, source_target_pairs={{0,8},{8,0},{1,9},{9,1},{2,10},{10,2},{3,11},{11,3},{4,12},{12,4},... | collective-permute-start | bytes 9437192 | tf_op jit(solution)/shard_map/ppermute | solution.py:51
  169.4 6.6 %collective-permute-start.6 = (bf16[8,3072]{1,0:T(8,128)(2,1)S(1)}, bf16[8,3072]{1,0:T(8,128)(2,1)S(1)}, u32[]{:S(2)}, u32[]{:S(2)}) collective-permute-start(bf16[8,3072]{1,0:T(8,128)(2,1)S(1)} %get-tuple-element.14), channel_id=1, source_target_pairs={{0,1},{1,0},{2,3},{3,2},{4,5},{5,4},{6,7},{7,6},{8,9},{9,8},{10,11... | collective-permute-start | bytes 147464 | tf_op jit(solution)/shard_map/ppermute | solution.py:84
  170.1 6.6 %collective-permute-start.7 = (bf16[8,3072]{1,0:T(8,128)(2,1)S(1)}, bf16[8,3072]{1,0:T(8,128)(2,1)S(1)}, u32[]{:S(2)}, u32[]{:S(2)}) collective-permute-start(bf16[8,3072]{1,0:T(8,128)(2,1)S(1)} %get-tuple-element.14), channel_id=1, source_target_pairs={{0,2},{1,3},{2,0},{3,1},{4,6},{5,7},{6,4},{7,5},{8,10},{9,11},{10,... | collective-permute-start | bytes 147464 | tf_op jit(solution)/shard_map/ppermute | solution.py:84
  173.6 5.3 %collective-permute-start.8 = (bf16[8,3072]{1,0:T(8,128)(2,1)S(1)}, bf16[8,3072]{1,0:T(8,128)(2,1)S(1)}, u32[]{:S(2)}, u32[]{:S(2)}) collective-permute-start(bf16[8,3072]{1,0:T(8,128)(2,1)S(1)} %get-tuple-element.14), channel_id=1, source_target_pairs={{0,3},{1,2},{2,1},{3,0},{4,7},{5,6},{6,5},{7,4},{8,11},{9,10},{10,... | collective-permute-start | bytes 147464 | tf_op jit(solution)/shard_map/ppermute | solution.py:84
  178.9 7.0 %collective-permute-start.10 = (bf16[8,3072]{1,0:T(8,128)(2,1)S(1)}, bf16[8,3072]{1,0:T(8,128)(2,1)S(1)}, u32[]{:S(2)}, u32[]{:S(2)}) collective-permute-start(bf16[8,3072]{1,0:T(8,128)(2,1)S(1)} %fusion.51), channel_id=1, source_target_pairs={{0,64},{4,68},{64,0},{68,4},{1,65},{5,69},{65,1},{69,5},{2,66},{6,... | collective-permute-start | bytes 147464 | tf_op jit(solution)/shard_map/ppermute | solution.py:84
  181.9 5.3 %collective-permute-start.11 = (bf16[8,3072]{1,0:T(8,128)(2,1)S(1)}, bf16[8,3072]{1,0:T(8,128)(2,1)S(1)}, u32[]{:S(2)}, u32[]{:S(2)}) collective-permute-start(bf16[8,3072]{1,0:T(8,128)(2,1)S(1)} %fusion.51), channel_id=1, source_target_pairs={{0,68},{4,64},{64,4},{68,0},{1,69},{5,65},{65,5},{69,1},{2,70},{6,... | collective-permute-start | bytes 147464 | tf_op jit(solution)/shard_map/ppermute | solution.py:84
  182.8 5.6 %collective-permute-start.9 = (bf16[8,3072]{1,0:T(8,128)(2,1)S(1)}, bf16[8,3072]{1,0:T(8,128)(2,1)S(1)}, u32[]{:S(2)}, u32[]{:S(2)}) collective-permute-start(bf16[8,3072]{1,0:T(8,128)(2,1)S(1)} %fusion.51), channel_id=1, source_target_pairs={{0,4},{4,0},{64,68},{68,64},{1,5},{5,1},{65,69},{69,65},{2,6},{6,2... | collective-permute-start | bytes 147464 | tf_op jit(solution)/shard_map/ppermute | solution.py:84
  188.4 4.1 %copy-start.14 = (f32[8,3072]{1,0:T(8,128)}, f32[8,3072]{1,0:T(8,128)S(1)}, u32[]{:S(2)}) copy-start(f32[8,3072]{1,0:T(8,128)S(1)} %add_add_fusion) | copy-start | bytes 294916
  192.5 7.2 %copy-start.10 = (bf16[1024,512]{1,0:T(8,128)(2,1)S(1)}, bf16[1024,512]{1,0:T(8,128)(2,1)}, u32[]{:S(2)}) copy-start(bf16[1024,512]{1,0:T(8,128)(2,1)} %copy-done.9) | copy-start | bytes 3145732
  192.5 46.7 %all-to-all-start.3 = ((bf16[64,8,3072]{2,1,0:T(8,128)(2,1)}), bf16[64,8,3072]{2,1,0:T(8,128)(2,1)}, u32[]{:S(2)}, u32[]{:S(2)}) async-start(bf16[64,8,3072]{2,1,0:T(8,128)(2,1)} %fusion.7), calls=%async_computation.3 | async-start | bytes 6291456 | tf_op jit(solution)/shard_map/all_to_all | solution.py:72
  199.7 7.8 %copy-start.13 = (bf16[8,3072]{1,0:T(8,128)(2,1)S(1)}, bf16[8,3072]{1,0:T(8,128)(2,1)}, u32[]{:S(2)}) copy-start(bf16[8,3072]{1,0:T(8,128)(2,1)} %param.8) | copy-start | bytes 147460
  199.7 8.1 %copy-start.8 = (bf16[1024,512]{1,0:T(8,128)(2,1)S(1)}, bf16[1024,512]{1,0:T(8,128)(2,1)}, u32[]{:S(2)}) copy-start(bf16[1024,512]{1,0:T(8,128)(2,1)} %copy-done.7) | copy-start | bytes 3145732
  199.7 16.0 %slice-start = ((s8[6291456]{0:T(1024)(128)(4,1)}), s8[4194304]{0:T(1024)(128)(4,1)S(1)}, s32[]{:S(2)}) async-start(s8[6291456]{0:T(1024)(128)(4,1)} %bitcast.106), calls=%async_computation.6 | async-start | bytes 8388608
  207.8 7.9 %copy-start.6 = (bf16[1024,512]{1,0:T(8,128)(2,1)S(1)}, bf16[1024,512]{1,0:T(8,128)(2,1)}, u32[]{:S(2)}) copy-start(bf16[1024,512]{1,0:T(8,128)(2,1)} %copy-done.5) | copy-start | bytes 3145732
  207.8 7.9 %slice-start.1 = ((s8[6291456]{0:T(1024)(128)(4,1)}), s8[2097152]{0:T(1024)(128)(4,1)S(1)}, s32[]{:S(2)}) async-start(s8[6291456]{0:T(1024)(128)(4,1)} %bitcast.106), calls=%async_computation.7 | async-start | bytes 4194304
  215.8 26.7 %copy-start.1 = (bf16[1,512,3072]{2,1,0:T(8,128)(2,1)S(1)}, bf16[1,512,3072]{2,1,0:T(8,128)(2,1)}, u32[]{:S(2)}) copy-start(bf16[1,512,3072]{2,1,0:T(8,128)(2,1)} %param.12) | copy-start | bytes 9437188
Sparse Core Ops, SparseCore 0:
  25.6 45.1 all-gather.2
  72.5 79.5 all-gather.4
